TPU v7x, 32 devices: a whole 2x2x4 slice. The times are simulated.
32 devices in a mesh: dp: 16 (over z, y, core), feat: 2 (over x).
Axes of the slice: x: 2, y: 2, z: 4, core: 2. Of those that a mesh axis runs over, the one named last changes fastest.
Arguments:
- embeddings: bfloat16 [32768, 1024], P('dp', 'feat')
- assignments: int32 [32768], P('dp'), may hold values from 0 to 127, as said below
- order_index: int32 [32768], P('dp'), may hold values from 0 to 32767, each once
- cluster_blocks: int32 [128], replicated, may hold values from 1 to 4, as said below
Outputs:
- centroids: bfloat16 [128, 1024], P('dp', 'feat')
- centroid_sim: float32 [32768], P('dp')
- earlier_max: float32 [32768], P('dp')
Inputs may be any that keep to these rules, and one draw needn't show every extreme that they name: `assignments`: every cluster holds at least one row. The rows of one index of dp name one cluster at most 32 times, and on every index some cluster exactly 32 times. `cluster_blocks`: the number of rows of the cluster divided by 128, rounded up; some cluster has 512 rows.
All inputs are finite; a program needn't handle non-finite values.
Results may differ from a plain program's by a relative error of at most 0.0012.
Values may be sent and summed in bfloat16 or wider, within the bound.
No kernel may reach another device: no remote copies, remote signals or barrier semaphores. Data moves between devices by JAX's collectives and lax.ppermute only.
A program may use at most 64 MiB of HBM per device.

v0:
```python
from functools import partial

import jax
import jax.numpy as jnp
from jax import lax
from jax.sharding import PartitionSpec as P

epsilon = 1e-06
block_rows = 128


def masked_best(unit_rows, row_order, used_rows):
    leading = unit_rows[:used_rows]
    key_order = row_order[:used_rows]
    similar = jnp.dot(leading, leading.T, preferred_element_type=jnp.float32)
    earlier = (key_order[None, :] < key_order[:, None]) & (key_order[None, :] >= 0)
    best_match = jnp.max(jnp.where(earlier, similar, jnp.float32(-1.0)), axis=1)
    filler = jnp.full((unit_rows.shape[0] - used_rows,), -1.0, jnp.float32)
    return jnp.concatenate([best_match, filler])


def cluster_best(unit_rows, row_order, blocks_used):
    capacity = unit_rows.shape[0]
    branches = [
        partial(masked_best, used_rows=(level + 1) * block_rows)
        for level in range(capacity // block_rows)
    ]
    return lax.switch(blocks_used - 1, branches, unit_rows, row_order)


def compact(got_rows, got_order):
    n_sources, n_clusters, per_source, width = got_rows.shape
    capacity = n_sources * per_source
    filled = got_order >= 0
    source_counts = jnp.sum(filled, axis=2)
    offsets = jnp.cumsum(source_counts, axis=0) - source_counts
    position = offsets[:, :, None] + jnp.arange(per_source, dtype=jnp.int32)[None, None, :]
    target = jnp.where(filled, position, -1).transpose(1, 0, 2).reshape(n_clusters, capacity)
    rows_by_cluster = got_rows.transpose(1, 0, 2, 3).reshape(n_clusters, capacity, width)
    order_by_cluster = got_order.transpose(1, 0, 2).reshape(n_clusters, capacity)
    placing = jnp.arange(capacity, dtype=jnp.int32)[None, :, None] == target[:, None, :]
    packed = jnp.einsum(
        "cdu,cuw->cdw",
        placing.astype(jnp.bfloat16),
        rows_by_cluster,
        preferred_element_type=jnp.float32,
    ).astype(jnp.bfloat16)
    packed_order = jnp.max(jnp.where(placing, order_by_cluster[:, None, :], -1), axis=2).astype(
        jnp.int32
    )
    return (packed, packed_order, placing)


def unpack(results, placing, n_sources, per_source):
    n_clusters = results.shape[0]
    back = jnp.sum(jnp.where(placing, results[:, :, None], jnp.float32(0.0)), axis=1)
    return back.reshape(n_clusters, n_sources, per_source).transpose(1, 0, 2)


def body(embeddings, assignments, order_index, cluster_blocks):
    n_owners = lax.axis_size("dp")
    clusters = cluster_blocks.shape[0]
    cl_local = clusters // n_owners
    rows_here = assignments.shape[0]
    local_width = embeddings.shape[1]
    per_source = 2 * rows_here // clusters
    capacity = n_owners * per_source
    n_slots = clusters * per_source
    my_owner = lax.axis_index("dp")
    row_block = min(512, rows_here)
    n_row_blocks = rows_here // row_block
    member = jnp.arange(clusters, dtype=jnp.int32)[:, None] == assignments[None, :]
    onehot = member.astype(jnp.bfloat16)
    partial_sums = jnp.dot(onehot, embeddings, preferred_element_type=jnp.float32)
    local_counts = jnp.sum(member, axis=1)
    partial_counts = local_counts.astype(jnp.float32)
    total_sums, total_counts = lax.psum((partial_sums, partial_counts), "dp")
    averages = total_sums / total_counts[:, None]
    centre_norms = lax.psum(jnp.sum(averages * averages, axis=1), "feat")
    centroids = (averages / jnp.sqrt(centre_norms + epsilon)[:, None]).astype(jnp.bfloat16)
    own_centroids = lax.dynamic_slice_in_dim(centroids, my_owner * cl_local, cl_local, 0)
    values = embeddings.astype(jnp.float32)
    row_centres = lax.dot_general(
        onehot, centroids, (((0,), (0,)), ((), ())), preferred_element_type=jnp.float32
    )
    square_part = jnp.sum(values * values, axis=1)
    product_part = jnp.sum(values * row_centres, axis=1)
    squares, products = lax.psum((square_part, product_part), "feat")
    lengths = jnp.sqrt(squares + epsilon)
    centroid_sim = products / lengths
    normed = (values / lengths[:, None]).astype(jnp.bfloat16)
    member_blocks = member.reshape(clusters, n_row_blocks, row_block)
    before = (jnp.arange(row_block)[:, None] < jnp.arange(row_block)[None, :]).astype(jnp.bfloat16)
    within = jnp.einsum(
        "kbr,rs->kbs",
        member_blocks.astype(jnp.bfloat16),
        before,
        preferred_element_type=jnp.float32,
    )
    block_totals = jnp.sum(member_blocks, axis=2)
    block_offsets = (jnp.cumsum(block_totals, axis=1) - block_totals).astype(jnp.float32)
    rank_table = (within + block_offsets[:, :, None]).reshape(clusters, rows_here)
    row_rank = jnp.sum(jnp.where(member, rank_table, jnp.float32(0.0)), axis=0).astype(jnp.int32)
    send_slot = assignments * per_source + row_rank
    slot_ids = jnp.arange(n_slots, dtype=jnp.int32)

    def place_block(block_index, carry):
        rows_acc, order_acc = carry
        start = block_index * row_block
        slot_piece = lax.dynamic_slice_in_dim(send_slot, start, row_block, 0)
        rows_piece = lax.dynamic_slice_in_dim(normed, start, row_block, 0)
        order_piece = lax.dynamic_slice_in_dim(order_index, start, row_block, 0)
        hits = slot_ids[:, None] == slot_piece[None, :]
        rows_acc = rows_acc + jnp.dot(
            hits.astype(jnp.bfloat16), rows_piece, preferred_element_type=jnp.float32
        )
        order_acc = jnp.maximum(
            order_acc, jnp.max(jnp.where(hits, order_piece[None, :], -1), axis=1)
        )
        return (rows_acc, order_acc)

    placed_rows, send_order = lax.fori_loop(
        0,
        n_row_blocks,
        place_block,
        (jnp.zeros((n_slots, local_width), jnp.float32), jnp.full((n_slots,), -1, jnp.int32)),
    )
    send_rows = placed_rows.astype(jnp.bfloat16)
    my_blocks = lax.dynamic_slice_in_dim(cluster_blocks, my_owner * cl_local, cl_local, 0)
    got_rows, got_order = (
        lax.all_to_all(
            send_rows.reshape(n_owners, cl_local * per_source, local_width),
            "dp",
            split_axis=0,
            concat_axis=0,
            tiled=True,
        ),
        lax.all_to_all(
            send_order.reshape(n_owners, cl_local * per_source),
            "dp",
            split_axis=0,
            concat_axis=0,
            tiled=True,
        ),
    )
    got_rows = got_rows.reshape(n_owners, cl_local, per_source, local_width)
    got_order = got_order.reshape(n_owners, cl_local, per_source)
    packed, packed_order, placing = compact(got_rows, got_order)

    def visit(cluster_index, results):
        slice_rows = lax.dynamic_index_in_dim(packed, cluster_index, 0, keepdims=False)
        full_rows = lax.all_gather(slice_rows, "feat", axis=1, tiled=True)
        key_order = lax.dynamic_index_in_dim(packed_order, cluster_index, 0, keepdims=False)
        best_match = cluster_best(full_rows, key_order, my_blocks[cluster_index])
        return lax.dynamic_update_index_in_dim(results, best_match, cluster_index, 0)

    results = lax.fori_loop(0, cl_local, visit, jnp.zeros((cl_local, capacity), jnp.float32))
    answer = unpack(results, placing, n_owners, per_source).reshape(n_owners, cl_local * per_source)
    returned = lax.all_to_all(answer, "dp", split_axis=0, concat_axis=0, tiled=True)
    returned_flat = returned.reshape(n_slots)

    def read_block(block_index):
        slot_piece = lax.dynamic_slice_in_dim(send_slot, block_index * row_block, row_block, 0)
        hits = slot_ids[:, None] == slot_piece[None, :]
        return jnp.sum(jnp.where(hits, returned_flat[:, None], jnp.float32(0.0)), axis=0)

    earlier_max = lax.map(read_block, jnp.arange(n_row_blocks, dtype=jnp.int32)).reshape(rows_here)
    return (own_centroids, centroid_sim, earlier_max)


def solution(mesh):
    return jax.shard_map(
        body,
        mesh=mesh,
        in_specs=(P("dp", "feat"), P("dp"), P("dp"), P()),
        out_specs=(P("dp", "feat"), P("dp"), P("dp")),
        check_vma=False,
    )
```

profile of v0, /device:TPU:0, one launch (start us, length us, event | category | flops | bytes accessed | tf_op | source)
XLA Modules:
  0.0 521.8 jit_solution(8646838173752338977)
XLA Ops:
  7.2 2.8 fusion.25
  11.6 2.9 copy.26
  14.6 35.0 %psum.36 = f32[128]{0:T(128)S(1)} all-reduce(f32[128]{0:T(128)S(1)} %convert_element_type.51), channel_id=1, replica_groups=mesh['dp'=16,'feat'=2] {'dp'}, use_global_device_ids=true, to_apply=%region_2.0 | all-reduce | flops 128 | bytes 1024 | tf_op jit(solution)/shard_map/psum | solution.py:77
  50.7 52.1 %all-reduce.6.cloned.1.call-done = f32[128,512]{1,0:T(8,128)} async-done(((f32[128,512]{1,0:T(8,128)}), f32[128,512]{1,0:T(8,128)}) %all-reduce.6.cloned.1.call-update) | async-done | bytes 262160 | tf_op jit(solution)/shard_map/psum | solution.py:77
  104.0 4.9 psum.37
  110.8 8.1 %all-reduce.3 = (f32[2048]{0:T(1024)S(1)}, f32[2048]{0:T(1024)S(1)}) all-reduce(f32[2048]{0:T(1024)S(1)} %fusion.18, f32[2048]{0:T(1024)S(1)} %fusion.19), channel_id=1, replica_groups=mesh['dp'=16,'feat'=2] {'feat'}, use_global_device_ids=true, to_apply=%region_6.0 | all-reduce | flops 4096 | bytes 32768 | tf_op jit(solution)/shard_map/psum | solution.py:88
  121.4 48.4 %while.44 = (s32[]{:T(128)}, f32[4096,512]{1,0:T(8,128)}, s32[4096]{0:T(1024)}, s32[2048]{0:T(1024)S(1)}, bf16[2048,512]{0,1:T(8,128)(2,1)}, /*index=5*/s32[2048...) while((s32[]{:T(128)}, f32[4096,512]{1,0:T(8,128)}, s32[4096]{0:T(1024)}, ...), condition=%wide.region_14.15_spmd.clone, body=%wide.region_12.14_spmd.clone.sunk | while | flops 2160070656 | bytes 17381552 | solution.py:122
  124.1 7.0 %select_add_fusion.2 = f32[4096,512]{1,0:T(8,128)} fusion(f32[4096,512]{1,0:T(8,128)} %get-tuple-element.596, s32[512]{0:T(512)S(1)} %dynamic_slice.106, pred[]{:T(512)S(6)} %compare.6, bf16[2048,512]{0,1:T(8,128)(2,1)} %get-tuple-element.609, s32[]{:T(128)S(6)} %select_n.117), kind=kOutput, calls=%fused_computation.22.clone.1 | convolution fusion | flops 2153775104 | bytes 17303556 | tf_op jit(solution)/shard_map/while/body/eval_jaxpr/dot_general | solution.py:114
  134.5 9.5 %select_add_fusion.2 = f32[4096,512]{1,0:T(8,128)} fusion(f32[4096,512]{1,0:T(8,128)} %get-tuple-element.596, s32[512]{0:T(512)S(1)} %dynamic_slice.106, pred[]{:T(512)S(6)} %compare.6, bf16[2048,512]{0,1:T(8,128)(2,1)} %get-tuple-element.609, s32[]{:T(128)S(6)} %select_n.117), kind=kOutput, calls=%fused_computation.22.clone.1 | convolution fusion | flops 2153775104 | bytes 17303556 | tf_op jit(solution)/shard_map/while/body/eval_jaxpr/dot_general | solution.py:114
  147.4 9.5 %select_add_fusion.2 = f32[4096,512]{1,0:T(8,128)} fusion(f32[4096,512]{1,0:T(8,128)} %get-tuple-element.596, s32[512]{0:T(512)S(1)} %dynamic_slice.106, pred[]{:T(512)S(6)} %compare.6, bf16[2048,512]{0,1:T(8,128)(2,1)} %get-tuple-element.609, s32[]{:T(128)S(6)} %select_n.117), kind=kOutput, calls=%fused_computation.22.clone.1 | convolution fusion | flops 2153775104 | bytes 17303556 | tf_op jit(solution)/shard_map/while/body/eval_jaxpr/dot_general | solution.py:114
  160.3 9.5 %select_add_fusion.2 = f32[4096,512]{1,0:T(8,128)} fusion(f32[4096,512]{1,0:T(8,128)} %get-tuple-element.596, s32[512]{0:T(512)S(1)} %dynamic_slice.106, pred[]{:T(512)S(6)} %compare.6, bf16[2048,512]{0,1:T(8,128)(2,1)} %get-tuple-element.609, s32[]{:T(128)S(6)} %select_n.117), kind=kOutput, calls=%fused_computation.22.clone.1 | convolution fusion | flops 2153775104 | bytes 17303556 | tf_op jit(solution)/shard_map/while/body/eval_jaxpr/dot_general | solution.py:114
  169.8 5.2 all-to-all-start
  175.0 5.9 %convert_element_type.60 = bf16[4096,512]{1,0:T(8,128)(2,1)} convert(f32[4096,512]{1,0:T(8,128)} %get-tuple-element.378) | non-fusion elementwise | flops 2097152 | bytes 12582912 | tf_op jit(solution)/shard_map/convert_element_type | solution.py:128
  181.5 5.6 %all-to-all-start.1 = ((bf16[16,256,512]{2,1,0:T(8,128)(2,1)}), bf16[16,256,512]{2,1,0:T(8,128)(2,1)}, u32[]{:S(2)}, u32[]{:S(2)}) async-start(bf16[16,256,512]{2,1,0:T(8,128)(2,1)} %bitcast.53), calls=%async_computation.1 | async-start | bytes 8388608 | tf_op jit(solution)/shard_map/all_to_all | solution.py:131
  189.4 75.3 %all-to-all-done.1 = bf16[16,256,512]{2,1,0:T(8,128)(2,1)} async-done(((bf16[16,256,512]{2,1,0:T(8,128)(2,1)}), bf16[16,256,512]{2,1,0:T(8,128)(2,1)}, u32[]{:S(2)}, u32[]{:S(2)}) %all-to-all-start.1) | async-done | bytes 4194336 | tf_op jit(solution)/shard_map/all_to_all | solution.py:131
  264.8 2.5 copy.29
  267.3 4.3 fusion.22
  271.6 218.3 %while.42 = (s32[]{:T(128)}, f32[8,512]{1,0:T(8,128)S(1)}, s32[8]{0:T(128)S(1)}, bf16[8,512,512]{2,1,0:T(8,128)(2,1)}, s32[8,512]{1,0:T(8,128)S(1)}, /*index=5*/...) while((s32[]{:T(128)}, f32[8,512]{1,0:T(8,128)S(1)}, s32[8]{0:T(128)S(1)}, ...), condition=%wide.region_27.28_spmd, body=%wide.region_18.27_spmd.sunk | while | flops 537919488 | bytes 6831409 | solution.py:157
  274.6 34.7 %all-gather.5.cloned.1.call-done = bf16[1,512,1024]{2,1,0:T(8,128)(2,1)} async-done(((bf16[1,512,512]{2,1,0:T(8,128)(2,1)}), bf16[1,512,1024]{2,1,0:T(8,128)(2,1)}) %all-gather.5.cloned.1.call-update) | async-done | bytes 1048592 | tf_op jit(solution)/shard_map/while/body/eval_jaxpr/all_gather | solution.py:152
  313.8 21.3 %all-gather.5.cloned.1.call-done = bf16[1,512,1024]{2,1,0:T(8,128)(2,1)} async-done(((bf16[1,512,512]{2,1,0:T(8,128)(2,1)}), bf16[1,512,1024]{2,1,0:T(8,128)(2,1)}) %all-gather.5.cloned.1.call-update) | async-done | bytes 1048592 | tf_op jit(solution)/shard_map/while/body/eval_jaxpr/all_gather | solution.py:152
  339.7 21.0 %all-gather.5.cloned.1.call-done = bf16[1,512,1024]{2,1,0:T(8,128)(2,1)} async-done(((bf16[1,512,512]{2,1,0:T(8,128)(2,1)}), bf16[1,512,1024]{2,1,0:T(8,128)(2,1)}) %all-gather.5.cloned.1.call-update) | async-done | bytes 1048592 | tf_op jit(solution)/shard_map/while/body/eval_jaxpr/all_gather | solution.py:152
  360.7 2.0 conditional.2
  365.9 19.9 %all-gather.5.cloned.1.call-done = bf16[1,512,1024]{2,1,0:T(8,128)(2,1)} async-done(((bf16[1,512,512]{2,1,0:T(8,128)(2,1)}), bf16[1,512,1024]{2,1,0:T(8,128)(2,1)}) %all-gather.5.cloned.1.call-update) | async-done | bytes 1048592 | tf_op jit(solution)/shard_map/while/body/eval_jaxpr/all_gather | solution.py:152
  390.6 20.7 %all-gather.5.cloned.1.call-done = bf16[1,512,1024]{2,1,0:T(8,128)(2,1)} async-done(((bf16[1,512,512]{2,1,0:T(8,128)(2,1)}), bf16[1,512,1024]{2,1,0:T(8,128)(2,1)}) %all-gather.5.cloned.1.call-update) | async-done | bytes 1048592 | tf_op jit(solution)/shard_map/while/body/eval_jaxpr/all_gather | solution.py:152
  415.9 21.3 %all-gather.5.cloned.1.call-done = bf16[1,512,1024]{2,1,0:T(8,128)(2,1)} async-done(((bf16[1,512,512]{2,1,0:T(8,128)(2,1)}), bf16[1,512,1024]{2,1,0:T(8,128)(2,1)}) %all-gather.5.cloned.1.call-update) | async-done | bytes 1048592 | tf_op jit(solution)/shard_map/while/body/eval_jaxpr/all_gather | solution.py:152
  442.0 21.1 %all-gather.5.cloned.1.call-done = bf16[1,512,1024]{2,1,0:T(8,128)(2,1)} async-done(((bf16[1,512,512]{2,1,0:T(8,128)(2,1)}), bf16[1,512,1024]{2,1,0:T(8,128)(2,1)}) %all-gather.5.cloned.1.call-update) | async-done | bytes 1048592 | tf_op jit(solution)/shard_map/while/body/eval_jaxpr/all_gather | solution.py:152
  463.0 2.0 conditional.2
  463.1 2.0 fusion.15
  468.3 19.9 %all-gather.5.cloned.1.call-done = bf16[1,512,1024]{2,1,0:T(8,128)(2,1)} async-done(((bf16[1,512,512]{2,1,0:T(8,128)(2,1)}), bf16[1,512,1024]{2,1,0:T(8,128)(2,1)}) %all-gather.5.cloned.1.call-update) | async-done | bytes 1048592 | tf_op jit(solution)/shard_map/while/body/eval_jaxpr/all_gather | solution.py:152
  492.0 5.6 %all-to-all-start.2 = ((f32[16,1,256]{2,1,0:T(1,128)}), f32[16,1,256]{2,1,0:T(1,128)S(1)}, u32[]{:S(2)}, u32[]{:S(2)}) async-start(f32[16,1,256]{2,1,0:T(1,128)} %all_to_all.23), calls=%async_computation.2 | async-start | bytes 32768 | tf_op jit(solution)/shard_map/all_to_all | solution.py:159
  498.2 5.9 %all-to-all-done.2 = f32[16,1,256]{2,1,0:T(1,128)S(1)} async-done(((f32[16,1,256]{2,1,0:T(1,128)}), f32[16,1,256]{2,1,0:T(1,128)S(1)}, u32[]{:S(2)}, u32[]{:S(2)}) %all-to-all-start.2) | async-done | bytes 16416 | tf_op jit(solution)/shard_map/all_to_all | solution.py:159
  504.1 10.6 %while.43 = (s32[]{:T(128)}, f32[4,512]{1,0:T(4,128)S(1)}, s32[4]{0:T(128)S(1)}, s32[2048]{0:T(1024)S(1)}, f32[16,256]{1,0:T(8,128)S(1)}, /*index=5*/s32[]{:T(128)}, s32[1]{0:T(128)}, s32[]{:T(128)}, s32[]{:T(128)}) while((s32[]{:T(128)}, f32[4,512]{1,0:T(4,128)S(1)}, s32[4]{0:T(128)S(1)}, s32[2048]{0:T(1024)S(1)}, ...), condition=%wide.region_31.32_spmd.clone, body=%wide.region_29.31_spmd.clone.sunk | while | flops 6290950 | bytes 61607 | solution.py:167
  (158 shorter events, 75.2 us)
Async XLA Ops:
  7.2 95.7 %all-reduce.6.cloned.1.call-start = ((), (), s32[]{:S(2)}) async-start(), calls=%async_computation.3 | async-start | bytes 524288 | tf_op jit(solution)/shard_map/psum | solution.py:77
  11.6 39.1 %copy-start = (s32[2048]{0:T(1024)S(1)}, s32[2048]{0:T(1024)}, u32[]{:S(2)}) copy-start(s32[2048]{0:T(1024)} %param.15) | copy-start | bytes 24580
  169.8 11.7 %all-to-all-start = ((s32[16,1,256]{2,1,0:T(1,128)}), s32[16,1,256]{2,1,0:T(1,128)S(1)}, u32[]{:S(2)}, u32[]{:S(2)}) async-start(s32[16,1,256]{2,1,0:T(1,128)} %bitcast.10), calls=%async_computation | async-start | bytes 32768 | tf_op jit(solution)/shard_map/all_to_all | solution.py:138
  181.5 5.6 %copy-start.1 = (s32[128]{0:T(128)S(1)}, s32[128]{0:T(128)}, u32[]{:S(2)}) copy-start(s32[128]{0:T(128)} %param.17) | copy-start | bytes 1540
  181.5 83.3 %all-to-all-start.1 = ((bf16[16,256,512]{2,1,0:T(8,128)(2,1)}), bf16[16,256,512]{2,1,0:T(8,128)(2,1)}, u32[]{:S(2)}, u32[]{:S(2)}) async-start(bf16[16,256,512]{2,1,0:T(8,128)(2,1)} %bitcast.53), calls=%async_computation.1 | async-start | bytes 8388608 | tf_op jit(solution)/shard_map/all_to_all | solution.py:131
  271.6 37.7 %all-gather.5.cloned.1.call-start = ((), (), s32[]{:S(2)}) async-start(), calls=%async_computation.4 | async-start | bytes 1572864 | tf_op jit(solution)/shard_map/while/body/eval_jaxpr/all_gather | solution.py:152
  310.7 24.5 %all-gather.5.cloned.1.call-start = ((), (), s32[]{:S(2)}) async-start(), calls=%async_computation.4 | async-start | bytes 1572864 | tf_op jit(solution)/shard_map/while/body/eval_jaxpr/all_gather | solution.py:152
  336.6 24.1 %all-gather.5.cloned.1.call-start = ((), (), s32[]{:S(2)}) async-start(), calls=%async_computation.4 | async-start | bytes 1572864 | tf_op jit(solution)/shard_map/while/body/eval_jaxpr/all_gather | solution.py:152
  362.8 23.0 %all-gather.5.cloned.1.call-start = ((), (), s32[]{:S(2)}) async-start(), calls=%async_computation.4 | async-start | bytes 1572864 | tf_op jit(solution)/shard_map/while/body/eval_jaxpr/all_gather | solution.py:152
  387.5 23.9 %all-gather.5.cloned.1.call-start = ((), (), s32[]{:S(2)}) async-start(), calls=%async_computation.4 | async-start | bytes 1572864 | tf_op jit(solution)/shard_map/while/body/eval_jaxpr/all_gather | solution.py:152
  412.7 24.5 %all-gather.5.cloned.1.call-start = ((), (), s32[]{:S(2)}) async-start(), calls=%async_computation.4 | async-start | bytes 1572864 | tf_op jit(solution)/shard_map/while/body/eval_jaxpr/all_gather | solution.py:152
  438.9 24.2 %all-gather.5.cloned.1.call-start = ((), (), s32[]{:S(2)}) async-start(), calls=%async_computation.4 | async-start | bytes 1572864 | tf_op jit(solution)/shard_map/while/body/eval_jaxpr/all_gather | solution.py:152
  465.2 23.0 %all-gather.5.cloned.1.call-start = ((), (), s32[]{:S(2)}) async-start(), calls=%async_computation.4 | async-start | bytes 1572864 | tf_op jit(solution)/shard_map/while/body/eval_jaxpr/all_gather | solution.py:152
  492.0 12.1 %all-to-all-start.2 = ((f32[16,1,256]{2,1,0:T(1,128)}), f32[16,1,256]{2,1,0:T(1,128)S(1)}, u32[]{:S(2)}, u32[]{:S(2)}) async-start(f32[16,1,256]{2,1,0:T(1,128)} %all_to_all.23), calls=%async_computation.2 | async-start | bytes 32768 | tf_op jit(solution)/shard_map/all_to_all | solution.py:159
Sparse Core Ops, SparseCore 0:
  11.4 91.4 all-reduce.5
  273.9 35.3 all-gather.4
  313.1 22.0 all-gather.4
  338.6 22.0 all-gather.4
  364.9 20.8 all-gather.4
  389.6 21.7 all-gather.4
  415.1 22.0 all-gather.4
  441.3 21.7 all-gather.4
  467.5 20.5 all-gather.4
where the time goes:
time: 524 us; the launch traced here: 522 us
  waiting for transfers between devices  314 us (60%)
  matrix products  56.2 us (11%)
  blocking collectives  48 us (9%)
  local copies, waits for them, and re-layouts  35.5 us (7%)
  other arithmetic  29.5 us (6%)
  starting transfers between devices  16.8 us (3%)
  between operations  13.9 us (3%)
  loops' own time  7.95 us (2%)
    all_gather x8, waiting for transfers between devices, visit(): full_rows = lax.all_gather(slice_rows, 'feat', axis=1, tiled=True)  180 us
    all_to_all x1, waiting for transfers between devices, body(): lax.all_to_all(send_rows.reshape(n_owners, cl_local * per_source, local_w...  75.3 us
    psum x1, waiting for transfers between devices, body(): total_sums, total_counts = lax.psum((partial_sums, partial_counts), 'dp')  52.1 us
    dot_general x4, matrix products, place_block(): jnp.dot(hits.astype(jnp.bfloat16), rows_piece, preferred_element_type=jnp...  35.4 us
    psum x1, blocking collectives, body(): total_sums, total_counts = lax.psum((partial_sums, partial_counts), 'dp')  35 us
    dynamic_slice x8, local copies, waits for them, and re-layouts, visit(): lax.dynamic_index_in_dim(packed, cluster_index, 0, keepdims=False)  15.1 us
    dot_general x8, matrix products, masked_best(): similar = jnp.dot(leading, leading.T, preferred_element_type=jnp.float32)  12.4 us
  transfers between devices with their start and end apart: 12, of which 12 were waited for; matrix products, arithmetic and copies ran while one was open for 4% of the time, Pallas kernels for 0%

commit v1 on v0

v1 whole, which is shorter than its diff:
```python
from functools import partial

import jax
import jax.numpy as jnp
from jax import lax
from jax.experimental import pallas as pl
from jax.experimental.pallas import tpu as pltpu
from jax.sharding import PartitionSpec as P

epsilon = 1e-06
lanes = 128
AXES = ("dp", "feat")
f32 = jnp.float32
bf16 = jnp.bfloat16
last_last = (((1,), (1,)), ((), ()))


def iota(shape, dim):
    return lax.broadcasted_iota(jnp.int32, shape, dim)


def pack_kernel(
    dests, slots, assign_ref, order_ref, blocks_ref, rows_ref, out_ref, info_ref, table_ref,
    flat_ref, pieces_ref, places_ref, meta_ref,
):
    clusters = blocks_ref.shape[1]
    rows = rows_ref.shape[0]
    width = rows_ref.shape[1]
    share = clusters // dests
    cap = slots - 1

    sort_key = (blocks_ref[...] * clusters + iota((1, clusters), 1)).astype(f32)
    key_cols = jnp.broadcast_to(sort_key, (clusters, clusters))
    key_rows = key_cols.T
    rank = jnp.sum(jnp.where(key_cols < key_rows, 1.0, 0.0), axis=1, keepdims=True)
    turn = sum(jnp.where(rank >= t * dests, 1.0, 0.0) for t in range(1, share))
    rest = rank - turn * dests
    odd = (turn == 1.0) | (turn == 3.0)
    dest_of = jnp.where(odd, dests - 1.0 - rest, rest)
    code_of = dest_of * share + turn
    table_ref[...] = jnp.broadcast_to(code_of, table_ref.shape).astype(jnp.int32)

    step = 2 * lanes
    before = (iota((step, step), 0) < iota((step, step), 1)).astype(f32).astype(bf16)
    taken = jnp.zeros((dests, 1), f32)
    for b in range(rows // step):
        at = pl.ds(b * step, step)
        assign = jnp.concatenate([assign_ref[2 * b : 2 * b + 1], assign_ref[2 * b + 1 : 2 * b + 2]], axis=1)
        order = jnp.concatenate([order_ref[2 * b : 2 * b + 1], order_ref[2 * b + 1 : 2 * b + 2]], axis=1)
        member = iota((clusters, step), 0) == assign
        code = jnp.sum(jnp.where(member, code_of, 0.0), axis=0, keepdims=True).astype(jnp.int32)
        dest = code // share
        turn_row = code - dest * share
        hit = iota((dests, step), 0) == dest
        hit_f = jnp.where(hit, 1.0, 0.0)
        ahead = jnp.dot(hit_f.astype(bf16), before, preferred_element_type=f32) + taken
        taken = taken + jnp.sum(hit_f, axis=1, keepdims=True)
        position = jnp.sum(jnp.where(hit, ahead, 0.0), axis=0, keepdims=True).astype(jnp.int32)
        info_ref[0:1, at] = dest
        info_ref[1:2, at] = position
        fits = position < cap
        flat_ref[0:1, at] = jnp.where(fits, dest * slots + position, -1)
        parts = (order & 127, (order >> 7) & 127, order >> 14, turn_row + 1)
        for q, part in enumerate(parts):
            pieces_ref[q * dests : (q + 1) * dests, at] = jnp.where(hit, part.astype(f32), 0.0).astype(bf16)
        places_ref[:, at] = jnp.where((iota((lanes, step), 0) == position) & fits, 1.0, 0.0).astype(bf16)

    meta = lax.dot_general(pieces_ref[...], places_ref[...], last_last, preferred_element_type=f32)
    if cap < lanes:
        most = jnp.max(taken, axis=0, keepdims=True)
        flagged = (iota(meta.shape, 0) >= 3 * dests) & (iota(meta.shape, 1) == lanes - 1)
        meta = jnp.where(flagged, most, meta)
    meta_ref[...] = meta

    group = max(1, 768 // slots)
    while dests % group:
        group -= 1
    flat = flat_ref[0:1, :]

    def place(g, _):
        base = g * group
        target = flat - base * slots
        hits = jnp.where(iota((group * slots, rows), 0) == target, 1.0, 0.0).astype(bf16)
        placed = jnp.dot(hits, rows_ref[...], preferred_element_type=f32)
        for j in range(group):
            note = jnp.concatenate(
                [meta_ref[pl.ds(q * dests + base + j, 1), :] for q in range(4)], axis=1
            )
            block = placed[j * slots : (j + 1) * slots]
            out_ref[base + j] = jnp.where(iota((slots, width), 0) == cap, note, block).astype(bf16)
        return 0

    lax.fori_loop(0, dests // group, place, 0)


def split3(value):
    high = value.astype(bf16).astype(f32)
    middle = (value - high).astype(bf16).astype(f32)
    return high, middle, value - high - middle


def owner_kernel(
    big, got_ref, back_ref, flag_ref, unit_ref, key_ref, low_ref, turn_ref, inverse_ref, row_key_ref, tile_ref, best_ref, centre_ref,
):
    blocks, slots, width = got_ref.shape
    sources = blocks // 2
    cap = slots - 1
    total = sources * slots
    lane = iota((1, lanes), 1)
    most = jnp.zeros((1, 1), f32)

    for s in range(sources):
        note = got_ref[2 * s, slots - 8 : slots, :].astype(f32)[7:8]
        turn = jnp.where(lane < cap, note[:, 3 * lanes : 4 * lanes], 0.0)
        order = note[:, :lanes] + 128.0 * note[:, lanes : 2 * lanes] + 16384.0 * note[:, 2 * lanes : 3 * lanes]
        if cap < lanes:
            most = jnp.maximum(most, note[:, 4 * lanes - 1 : 4 * lanes])
        turn_ref[s : s + 1, :] = turn
        key = jnp.where(turn > 0.0, turn * big + order, 0.0)
        tile_ref[s : s + 1, :] = key
        reach = min(slots, lanes)
        row_key_ref[0:1, s * slots : s * slots + reach] = key[:, :reach]
        if reach < slots:
            row_key_ref[0:1, s * slots + reach : (s + 1) * slots] = jnp.zeros((1, slots - reach), f32)
    flag_ref[...] = jnp.broadcast_to(jnp.where(most > cap, 1, 0), flag_ref.shape).astype(jnp.int32)
    key_cols = tile_ref[...].T
    turn_cols = turn_ref[...].T

    sums = [jnp.zeros((8, width), f32) for _ in range(2)]
    counts = jnp.zeros((8, 1), f32)
    for s in range(sources):
        at = pl.ds(s * slots, slots)
        key_col = key_cols[: min(slots, lanes), s : s + 1]
        turn_col = turn_cols[: min(slots, lanes), s : s + 1]
        turn_row = turn_ref[s : s + 1, : min(slots, lanes)]
        if slots > lanes:
            filler = jnp.zeros((slots - lanes, 1), f32)
            key_col = jnp.concatenate([key_col, filler], axis=0)
            turn_col = jnp.concatenate([turn_col, filler], axis=0)
        key_ref[at, :] = jnp.broadcast_to(key_col, (slots, lanes))
        low_ref[at, :] = jnp.broadcast_to(turn_col, (slots, lanes))
        first = got_ref[2 * s].astype(f32)
        second = got_ref[2 * s + 1].astype(f32)
        squares = jnp.sum(first * first + second * second, axis=1, keepdims=True)
        inverse = 1.0 / jnp.sqrt(squares + epsilon)
        inverse_ref[at, :] = jnp.broadcast_to(inverse, (slots, lanes))
        unit_ref[at, :width] = (first * inverse).astype(bf16)
        unit_ref[at, width:] = (second * inverse).astype(bf16)
        reach = min(slots, lanes)
        member = jnp.where(iota((8, reach), 0).astype(f32) == turn_row - 1.0, 1.0, 0.0)
        counts = counts + jnp.sum(member, axis=1, keepdims=True)
        member = member.astype(bf16)
        for f in range(2):
            sums[f] = sums[f] + jnp.dot(
                member, got_ref[2 * s + f, :reach, :], preferred_element_type=f32
            )

    counts = jnp.where(counts > 0.0, counts, 1.0)
    averages = [part / counts for part in sums]
    norms = jnp.sum(averages[0] * averages[0] + averages[1] * averages[1], axis=1, keepdims=True)
    lengths = jnp.sqrt(norms + epsilon)
    centres = [part / lengths for part in averages]
    for f in range(2):
        for j in range(4):
            for h in range(2):
                centre_ref[f, 2 * j + h : 2 * j + h + 1, :] = centres[f][j : j + 1, h * 256 : (h + 1) * 256]
    centres = [part.astype(bf16) for part in centres]

    group = max(1, 384 // slots)
    while sources % group:
        group -= 1
    span = group * slots

    def compare(g, _):
        start = pl.multiple_of(g * span, 8)
        mine = unit_ref[pl.ds(start, span), :]
        similar = lax.dot_general(mine, unit_ref[...], last_last, preferred_element_type=f32)
        own = key_ref[pl.ds(start, span), :][:, :1]
        low = low_ref[pl.ds(start, span), :][:, :1] * big
        other = row_key_ref[...]
        earlier = (other >= low) & (other < own)
        best = jnp.max(jnp.where(earlier, similar, -1.0), axis=1, keepdims=True)
        best_ref[pl.ds(start, span), :] = jnp.broadcast_to(best, (span, lanes))
        return 0

    lax.fori_loop(0, sources // group, compare, 0)

    lane_wide = iota((slots, lanes), 1)
    for s in range(sources):
        at = pl.ds(s * slots, slots)
        product = sum(
            lax.dot_general(got_ref[2 * s + f], centres[f], last_last, preferred_element_type=f32)
            for f in range(2)
        )
        chosen = iota((slots, 8), 1).astype(f32) == low_ref[at, :][:, :1] - 1.0
        cosine = jnp.sum(jnp.where(chosen, product, 0.0), axis=1, keepdims=True) * inverse_ref[at, :][:, :1]
        both = jnp.where(lane_wide == 0, cosine, best_ref[at, :])
        tile_ref[: min(slots, lanes), :] = both[:lanes]
        across = tile_ref[...].T
        parts = split3(across[0:1]) + split3(across[1:2])
        row = iota((8, lanes), 0)
        answer = jnp.zeros((8, lanes), f32)
        for t, part in enumerate(parts):
            answer = jnp.where(row == t, part, answer)
        for f in range(2):
            back_ref[2 * s + f] = jnp.concatenate([centre_ref[f], answer], axis=1).astype(bf16)


def return_kernel(share, mine_ref, back_ref, info_ref, table_ref, centre_ref, cosine_ref, best_ref):
    dests = back_ref.shape[0]
    rows = info_ref.shape[1]
    step = 4 * lanes
    answers = back_ref[:, :, 256:].reshape(dests * 8, lanes)
    for b in range(rows // step):
        at = pl.ds(b * step, step)
        dest = info_ref[0:1, at]
        position = info_ref[1:2, at]
        place = jnp.where(iota((lanes, step), 0) == position, 1.0, 0.0).astype(bf16)
        picked = jnp.dot(answers, place, preferred_element_type=f32)
        picked = jnp.where(iota((dests * 8, step), 0) // 8 == dest, picked, 0.0)
        picked = jnp.sum(picked.reshape(dests, 8, step), axis=0)
        cosine = picked[0:1] + picked[1:2] + picked[2:3]
        best = picked[3:4] + picked[4:5] + picked[5:6]
        for c in range(step // lanes):
            row = b * (step // lanes) + c
            cosine_ref[row : row + 1, :] = cosine[:, c * lanes : (c + 1) * lanes]
            best_ref[row : row + 1, :] = best[:, c * lanes : (c + 1) * lanes]
    owned = centre_ref.shape[0]
    code = table_ref[pl.ds(pl.multiple_of(mine_ref[0] * owned, 8), owned), :][:, :1]
    dest = code // share
    turn = code - dest * share
    stored = back_ref[:, :, :256].reshape(dests * 8, 256)
    for h in range(2):
        want = dest * 8 + 2 * turn + h
        hits = jnp.where(iota((owned, dests * 8), 1) == want, 1.0, 0.0).astype(bf16)
        centre_ref[:, h * 256 : (h + 1) * 256] = jnp.dot(
            hits, stored, preferred_element_type=f32
        ).astype(bf16)


def vmem(count):
    return [pl.BlockSpec(memory_space=pltpu.VMEM)] * count


params = pltpu.CompilerParams(vmem_limit_bytes=50 * 1024 * 1024)


def exchange(x):
    return lax.all_to_all(x, AXES, split_axis=0, concat_axis=0, tiled=True)


def route(slots, embeddings, assignments, order_index, cluster_blocks):
    n_dp = lax.axis_size("dp")
    dests = n_dp * lax.axis_size("feat")
    rows, width = embeddings.shape
    clusters = cluster_blocks.shape[0]
    share = clusters // dests
    total = n_dp * slots
    big = float(n_dp * rows)

    sent, info, table = pl.pallas_call(
        partial(pack_kernel, dests, slots),
        out_shape=(
            jax.ShapeDtypeStruct((dests, slots, width), bf16),
            jax.ShapeDtypeStruct((8, rows), jnp.int32),
            jax.ShapeDtypeStruct((clusters, lanes), jnp.int32),
        ),
        in_specs=vmem(4),
        out_specs=tuple(vmem(3)),
        scratch_shapes=[
            pltpu.VMEM((8, rows), jnp.int32),
            pltpu.VMEM((4 * dests, rows), bf16),
            pltpu.VMEM((lanes, rows), bf16),
            pltpu.VMEM((4 * dests, lanes), f32),
        ],
        compiler_params=params,
        name="pack",
    )(
        assignments.reshape(rows // lanes, lanes),
        order_index.reshape(rows // lanes, lanes),
        cluster_blocks.reshape(1, clusters),
        embeddings,
    )
    got = exchange(sent)
    back, flag = pl.pallas_call(
        partial(owner_kernel, big),
        out_shape=(
            jax.ShapeDtypeStruct((dests, 8, 384), bf16),
            jax.ShapeDtypeStruct((8, lanes), jnp.int32),
        ),
        in_specs=vmem(1),
        out_specs=tuple(vmem(2)),
        scratch_shapes=[
            pltpu.VMEM((total, 2 * width), bf16),
            pltpu.VMEM((total, lanes), f32),
            pltpu.VMEM((total, lanes), f32),
            pltpu.VMEM((lanes, lanes), f32),
            pltpu.VMEM((total, lanes), f32),
            pltpu.VMEM((1, total), f32),
            pltpu.VMEM((lanes, lanes), f32),
            pltpu.VMEM((total, lanes), f32),
            pltpu.VMEM((2, 8, 256), f32),
        ],
        compiler_params=params,
        name="owner",
    )(got)
    returned = exchange(back)
    mine = lax.axis_index("dp").reshape(1).astype(jnp.int32)
    centres, cosine, best = pl.pallas_call(
        partial(return_kernel, share),
        out_shape=(
            jax.ShapeDtypeStruct((clusters // n_dp, width), bf16),
            jax.ShapeDtypeStruct((rows // lanes, lanes), f32),
            jax.ShapeDtypeStruct((rows // lanes, lanes), f32),
        ),
        in_specs=[pl.BlockSpec(memory_space=pltpu.SMEM)] + vmem(3),
        out_specs=tuple(vmem(3)),
        compiler_params=params,
        name="answers",
    )(mine, returned, info, table)
    return (centres, cosine.reshape(rows), best.reshape(rows)), flag[0, 0] > 0


def body(embeddings, assignments, order_index, cluster_blocks):
    dests = lax.axis_size("dp") * lax.axis_size("feat")
    rows = assignments.shape[0]
    clusters = cluster_blocks.shape[0]
    most = (clusters // dests) * (2 * rows // clusters)
    args = (embeddings, assignments, order_index, cluster_blocks)
    outputs, over = route(3 * most // 4, *args)
    return lax.cond(over, lambda: route(most + 8, *args)[0], lambda: outputs)


def solution(mesh):
    return jax.shard_map(
        body,
        mesh=mesh,
        in_specs=(P("dp", "feat"), P("dp"), P("dp"), P()),
        out_specs=(P("dp", "feat"), P("dp"), P("dp")),
        check_vma=False,
    )
```

time: 524 us -> 116 us (0.22)
  waiting for transfers between devices: 314 us -> 8.49 us
  matrix products: 56.2 us -> 0 us
  local copies, waits for them, and re-layouts: 35.5 us -> 0.53 us
  blocking collectives: 48 us -> 78.3 us
  other arithmetic: 29.5 us -> 0 us
  Pallas kernels: 0 us -> 23.2 us
  starting transfers between devices: 16.8 us -> 3.66 us
  between operations: 13.9 us -> 1.5 us
  loops' own time: 7.95 us -> 0.23 us
    all_gather x8 -> x0, waiting for transfers between devices: 180 us -> none  [visit(): full_rows = lax.all_gather(slice_rows, 'feat', axis=1, tiled=True)]
    all_to_all x0 -> x1, blocking collectives: none -> 78.3 us  [exchange(): return lax.all_to_all(x, AXES, split_axis=0, concat_axis=0, tiled=True)]
    all_to_all x3 -> x1, waiting for transfers between devices: 81.8 us -> 8.49 us  [exchange(): return lax.all_to_all(x, AXES, split_axis=0, concat_axis=0, tiled=True)]
    dot_general x16 -> x0, matrix products: 56.2 us -> none  [the longest x4 35.4 us: place_block(): jnp.dot(hits.astype(jnp.bfloat16), rows_piece, preferred_element_type=jnp...]
    psum x1 -> x0, waiting for transfers between devices: 52.1 us -> none  [body(): total_sums, total_counts = lax.psum((partial_sums, partial_counts), 'dp')]
    psum x3 -> x0, blocking collectives: 48 us -> none  [the longest x1 35 us: body(): total_sums, total_counts = lax.psum((partial_sums, partial_counts), 'dp')]
    dynamic_slice x34 -> x0, local copies, waits for them, and re-layouts: 26.8 us -> none  [the longest x8 15.1 us: visit(): lax.dynamic_index_in_dim(packed, cluster_index, 0, keepdims=False)]
    pallas_call x0 -> x3, Pallas kernels: none -> 23.2 us  [the longest x1 12.5 us: route(): pl.pallas_call(partial(owner_kernel, big), out_shape=(jax.ShapeDtypeStruc...]
  transfers between devices with their start and end apart: 12 -> 1, of which waited for: 12 -> 1; matrix products, arithmetic and copies ran while one was open for 4% -> 0% of each run, Pallas kernels for 0% -> 0%
where the time goes in v1:
time: 116 us
  blocking collectives  78.3 us (68%)
  Pallas kernels  23.2 us (20%)
  waiting for transfers between devices  8.49 us (7%)
  starting transfers between devices  3.66 us (3%)
  between operations  1.5 us (1%)
    all_to_all x1, blocking collectives, exchange(): return lax.all_to_all(x, AXES, split_axis=0, concat_axis=0, tiled=True)  78.3 us
    pallas_call x1, Pallas kernels, route(): pl.pallas_call(partial(owner_kernel, big), out_shape=(jax.ShapeDtypeStruc...  12.5 us
    pallas_call x1, Pallas kernels, route(): pl.pallas_call(partial(pack_kernel, dests, slots), out_shape=(jax.ShapeDt...  9.7 us
    all_to_all x1, waiting for transfers between devices, exchange(): return lax.all_to_all(x, AXES, split_axis=0, concat_axis=0, tiled=True)  8.49 us
    all_to_all x1, starting transfers between devices, exchange(): return lax.all_to_all(x, AXES, split_axis=0, concat_axis=0, tiled=True)  3.66 us
  transfers between devices with their start and end apart: 1, of which 1 were waited for; matrix products, arithmetic and copies ran while one was open for 0% of the time, Pallas kernels for 0%

profile of v1, /device:TPU:0, one launch (start us, length us, event | category | flops | bytes accessed | tf_op | source)
XLA Modules:
  0.0 115.9 jit_solution(18025157177169569635)
XLA Ops:
  0.6 9.7 %pack.3 = (bf16[32,96,512]{2,1,0:T(8,128)(2,1)S(1)}, s32[8,2048]{1,0:T(8,128)S(1)}, s32[128,128]{1,0:T(8,128)S(1)}) custom-call(s32[16,128]{1,0:T(8,128)} %bitcast.11, s32[16,128]{1,0:T(8,128)} %bitcast.13, s32[1,128]{1,0:T(1,128)} %bitcast.15, bf16[2048,512]{1,0:T(8,128)(2,1)} %rows_ref.1), custom_call_target="tpu_custom_call" | custom-call | tf_op jit(solution)/shard_map/pack/pallas_call | solution.py:261
  10.3 78.3 %all_to_all.19.got_ref = bf16[32,96,512]{2,1,0:T(8,128)(2,1)S(1)} all-to-all(bf16[32,96,512]{2,1,0:T(8,128)(2,1)S(1)} %get-tuple-element.44), channel_id=1, replica_groups=mesh['dp'=16,'feat'=2] {'dp','feat'}, dimensions={0} | all-to-all | bytes 6291456 | tf_op jit(solution)/shard_map/all_to_all | solution.py:249
  88.6 0.0 copy-start
  88.6 0.0 copy-start.1
  88.6 0.0 copy-start.2
  88.6 0.0 copy-start.3
  88.6 12.5 %owner.3 = (bf16[32,8,384]{2,1,0:T(8,128)(2,1)}, s32[8,128]{1,0:T(8,128)S(1)}) custom-call(bf16[32,96,512]{2,1,0:T(8,128)(2,1)S(1)} %all_to_all.19.got_ref), custom_call_target="tpu_custom_call" | custom-call | tf_op jit(solution)/shard_map/owner/pallas_call | solution.py:285
  101.1 3.7 %all-to-all-start.3 = ((bf16[32,8,384]{2,1,0:T(8,128)(2,1)}), bf16[32,8,384]{2,1,0:T(8,128)(2,1)S(1)}, u32[]{:S(2)}, u32[]{:S(2)}) async-start(bf16[32,8,384]{2,1,0:T(8,128)(2,1)} %get-tuple-element.46), calls=%async_computation.3 | async-start | bytes 393216 | tf_op jit(solution)/shard_map/all_to_all | solution.py:249
  104.8 0.5 slice.3
  105.9 8.5 %all-to-all-done.3.back_ref = bf16[32,8,384]{2,1,0:T(8,128)(2,1)S(1)} async-done(((bf16[32,8,384]{2,1,0:T(8,128)(2,1)}), bf16[32,8,384]{2,1,0:T(8,128)(2,1)S(1)}, u32[]{:S(2)}, u32[]{:S(2)}) %all-to-all-start.3) | async-done | bytes 196640 | tf_op jit(solution)/shard_map/all_to_all | solution.py:249
  114.4 1.1 answers.3
  115.5 0.0 copy-done
  115.5 0.0 copy-done.1
  115.5 0.0 copy-done.2
  115.5 0.0 copy-done.3
  115.5 0.2 conditional.1
Async XLA Ops:
  88.6 26.9 %copy-start = (bf16[2048,512]{1,0:T(8,128)(2,1)S(1)}, bf16[2048,512]{1,0:T(8,128)(2,1)}, u32[]{:S(2)}) copy-start(bf16[2048,512]{1,0:T(8,128)(2,1)} %rows_ref.1) | copy-start | bytes 6291460
  88.6 26.9 %copy-start.1 = (s32[2048]{0:T(1024)S(1)}, s32[2048]{0:T(1024)}, u32[]{:S(2)}) copy-start(s32[2048]{0:T(1024)} %param.7) | copy-start | bytes 24580
  88.6 26.9 %copy-start.2 = (s32[2048]{0:T(1024)S(1)}, s32[2048]{0:T(1024)}, u32[]{:S(2)}) copy-start(s32[2048]{0:T(1024)} %param.8) | copy-start | bytes 24580
  88.6 26.9 %copy-start.3 = (s32[128]{0:T(128)S(1)}, s32[128]{0:T(128)}, u32[]{:S(2)}) copy-start(s32[128]{0:T(128)} %param.9) | copy-start | bytes 1540
  101.1 13.3 %all-to-all-start.3 = ((bf16[32,8,384]{2,1,0:T(8,128)(2,1)}), bf16[32,8,384]{2,1,0:T(8,128)(2,1)S(1)}, u32[]{:S(2)}, u32[]{:S(2)}) async-start(bf16[32,8,384]{2,1,0:T(8,128)(2,1)} %get-tuple-element.46), calls=%async_computation.3 | async-start | bytes 393216 | tf_op jit(solution)/shard_map/all_to_all | solution.py:249

commit v2 on v1

v2 whole, which is shorter than its diff:
```python
from functools import partial

import jax
import jax.numpy as jnp
from jax import lax
from jax.experimental import pallas as pl
from jax.experimental.pallas import tpu as pltpu
from jax.sharding import PartitionSpec as P

epsilon = 1e-06
lanes = 128
band = 32
chunk = 512
AXES = ("dp", "feat")
f32 = jnp.float32
bf16 = jnp.bfloat16
last_last = (((1,), (1,)), ((), ()))


def iota(shape, dim):
    return lax.broadcasted_iota(jnp.int32, shape, dim)


def pack_kernel(
    dests, slots, assign_ref, order_ref, blocks_ref, rows_hbm, out_ref, info_ref, table_ref,
    rows_ref, pieces_ref, places_ref, hits_ref, total_ref, copy_sem,
):
    clusters = blocks_ref.shape[1]
    rows, width = rows_ref.shape
    share = clusters // dests
    cap = slots - 1
    tall = places_ref.shape[0]
    copy = pltpu.make_async_copy(rows_hbm, rows_ref, copy_sem)
    copy.start()

    sort_key = (blocks_ref[...] * clusters + iota((1, clusters), 1)).astype(f32)
    key_cols = jnp.broadcast_to(sort_key, (clusters, clusters))
    key_rows = key_cols.T
    rank = jnp.sum(jnp.where(key_cols < key_rows, 1.0, 0.0), axis=1, keepdims=True)
    turn = sum(jnp.where(rank >= t * dests, 1.0, 0.0) for t in range(1, share))
    rest = rank - turn * dests
    odd = (turn == 1.0) | (turn == 3.0)
    dest_of = jnp.where(odd, dests - 1.0 - rest, rest)
    code_of = dest_of * share + turn
    table_ref[...] = jnp.broadcast_to(code_of, table_ref.shape).astype(jnp.int32)

    step = 2 * lanes
    before = (iota((step, step), 0) < iota((step, step), 1)).astype(f32).astype(bf16)
    taken = jnp.zeros((dests, 1), f32)
    reach = []
    for b in range(rows // step):
        at = pl.ds(b * step, step)
        assign = jnp.concatenate([assign_ref[2 * b : 2 * b + 1], assign_ref[2 * b + 1 : 2 * b + 2]], axis=1)
        order = jnp.concatenate([order_ref[2 * b : 2 * b + 1], order_ref[2 * b + 1 : 2 * b + 2]], axis=1)
        member = iota((clusters, step), 0) == assign
        code = jnp.sum(jnp.where(member, code_of, 0.0), axis=0, keepdims=True).astype(jnp.int32)
        dest = code // share
        turn_row = code - dest * share
        hit = iota((dests, step), 0) == dest
        hit_f = jnp.where(hit, 1.0, 0.0)
        hits_ref[:, at] = hit_f
        ahead = jnp.dot(hit_f.astype(bf16), before, preferred_element_type=f32) + taken
        if b * step % chunk == 0:
            low = jnp.min(taken)
        taken = taken + jnp.sum(hit_f, axis=1, keepdims=True)
        if (b + 1) * step % chunk == 0:
            reach.append((low, jnp.max(taken)))
        position = jnp.sum(jnp.where(hit, ahead, 0.0), axis=0, keepdims=True).astype(jnp.int32)
        info_ref[0:1, at] = dest
        info_ref[1:2, at] = position
        fits = position < cap
        parts = (order & 127, (order >> 7) & 127, order >> 14, turn_row + 1)
        for q, part in enumerate(parts):
            pieces_ref[q * dests : (q + 1) * dests, at] = jnp.where(hit, part.astype(f32), 0.0).astype(bf16)
        places_ref[:, at] = jnp.where((iota((tall, step), 0) == position) & fits, 1.0, 0.0).astype(bf16)

    meta = lax.dot_general(pieces_ref[...], places_ref[:lanes, :], last_last, preferred_element_type=f32)
    if cap < lanes:
        most = jnp.max(taken, axis=0, keepdims=True)
        flagged = (iota(meta.shape, 0) >= 3 * dests) & (iota(meta.shape, 1) == lanes - 1)
        meta = jnp.where(flagged, most, meta)
    copy.wait()

    note = jnp.concatenate([meta[q * dests : (q + 1) * dests] for q in range(4)], axis=1)
    for p in range(0, slots, band):
        begin = sum(jnp.where(high <= p, 1, 0) for _, high in reach)
        end = sum(jnp.where(low < p + band, 1, 0) for low, _ in reach)
        total_ref[...] = jnp.zeros_like(total_ref)

        def add(c, _):
            at = pl.ds(pl.multiple_of(c * chunk, chunk), chunk)
            place = places_ref[p : p + band, at].astype(f32)
            hits = hits_ref[:, at][:, None, :] * place[None, :, :]
            hits = hits.reshape(dests * band, chunk).astype(bf16)
            total_ref[...] += jnp.dot(hits, rows_ref[at, :], preferred_element_type=f32)
            return 0

        lax.fori_loop(begin, end, add, 0)
        block = total_ref[...].reshape(dests, band, width)
        if p + band == slots:
            block = jnp.where(iota((dests, band, width), 1) == band - 1, note[:, None, :], block)
        out_ref[:, p : p + band, :] = block.astype(bf16)


def split3(value):
    high = value.astype(bf16).astype(f32)
    middle = (value - high).astype(bf16).astype(f32)
    return high, middle, value - high - middle


def owner_kernel(
    got_ref, back_ref, flag_ref, unit_ref, inverse_ref, order_ref, turn_ref, row_order_ref, row_turn_ref, row_best_ref, centre_ref,
):
    blocks, slots, width = got_ref.shape
    sources = blocks // 2
    cap = slots - 1
    reach = min(slots, lanes)
    lane = iota((1, lanes), 1)
    most = jnp.zeros((1, 1), f32)

    order_ref[...] = jnp.zeros_like(order_ref)
    turn_ref[...] = jnp.zeros_like(turn_ref)
    row_best_ref[...] = jnp.full(row_best_ref.shape, -1.0, f32)
    if reach < slots:
        row_turn_ref[...] = jnp.zeros_like(row_turn_ref)
        row_order_ref[...] = jnp.zeros_like(row_order_ref)
    for s in range(sources):
        note = got_ref[2 * s, slots - band : slots, :].astype(f32)[band - 1 :]
        turn = jnp.where(lane < cap, note[:, 3 * lanes : 4 * lanes], 0.0)
        order = note[:, :lanes] + 128.0 * note[:, lanes : 2 * lanes] + 16384.0 * note[:, 2 * lanes : 3 * lanes]
        if cap < lanes:
            most = jnp.maximum(most, note[:, 4 * lanes - 1 : 4 * lanes])
        turn_ref[s : s + 1, :] = turn
        order_ref[s : s + 1, :] = order
        row_turn_ref[0:1, s * slots : s * slots + reach] = turn[:, :reach]
        row_order_ref[0:1, s * slots : s * slots + reach] = order[:, :reach]
    flag_ref[...] = jnp.broadcast_to(jnp.where(most > cap, 1, 0), flag_ref.shape).astype(jnp.int32)
    order_cols = order_ref[...].T
    turn_cols = turn_ref[...].T

    def column(table, s):
        col = table[:reach, s : s + 1]
        if reach < slots:
            col = jnp.concatenate([col, jnp.zeros((slots - reach, 1), f32)], axis=0)
        return col

    group = max(1, 384 // slots)
    while sources % group:
        group -= 1
    span = group * slots
    sums = [jnp.zeros((8, width), f32) for _ in range(2)]
    counts = jnp.zeros((8, 1), f32)
    bests = []
    for g in range(sources // group):
        mine = pl.ds(g * span, span)
        for s in range(g * group, (g + 1) * group):
            at = pl.ds(s * slots, slots)
            first = got_ref[2 * s].astype(f32)
            second = got_ref[2 * s + 1].astype(f32)
            squares = jnp.sum(first * first + second * second, axis=1, keepdims=True)
            inverse = 1.0 / jnp.sqrt(squares + epsilon)
            inverse_ref[at, :] = inverse
            unit_ref[at, :width] = (first * inverse).astype(bf16)
            unit_ref[at, width:] = (second * inverse).astype(bf16)
            member = jnp.where(
                iota((8, reach), 0).astype(f32) == turn_ref[s : s + 1, :reach] - 1.0, 1.0, 0.0
            )
            counts = counts + jnp.sum(member, axis=1, keepdims=True)
            member = member.astype(bf16)
            for f in range(2):
                sums[f] = sums[f] + jnp.dot(
                    member, got_ref[2 * s + f, :reach, :], preferred_element_type=f32
                )
        turn_col = jnp.concatenate([column(turn_cols, s) for s in range(g * group, (g + 1) * group)], axis=0)
        order_col = jnp.concatenate([column(order_cols, s) for s in range(g * group, (g + 1) * group)], axis=0)
        units = unit_ref[mine, :]
        best = jnp.full((span, 1), -1.0, f32)
        for h in range(g + 1):
            theirs = pl.ds(h * span, span)
            similar = lax.dot_general(units, unit_ref[theirs, :], last_last, preferred_element_type=f32)
            similar = jnp.where(turn_col == row_turn_ref[0:1, theirs], similar, -1.0)
            earlier = row_order_ref[0:1, theirs] < order_col
            best = jnp.maximum(best, jnp.max(jnp.where(earlier, similar, -1.0), axis=1, keepdims=True))
            if h < g:
                other = jnp.max(jnp.where(earlier, -1.0, similar), axis=0, keepdims=True)
                row_best_ref[0:1, theirs] = jnp.maximum(row_best_ref[0:1, theirs], other)
        bests.append(best)

    counts = jnp.where(counts > 0.0, counts, 1.0)
    averages = [part / counts for part in sums]
    norms = jnp.sum(averages[0] * averages[0] + averages[1] * averages[1], axis=1, keepdims=True)
    lengths = jnp.sqrt(norms + epsilon)
    centres = [part / lengths for part in averages]
    for f in range(2):
        for j in range(4):
            for h in range(2):
                centre_ref[f, 2 * j + h : 2 * j + h + 1, :] = centres[f][j : j + 1, h * 256 : (h + 1) * 256]
    centres = [part.astype(bf16) for part in centres]

    cosines = jnp.zeros((reach, lanes), f32)
    table = jnp.zeros((reach, lanes), f32)
    lane_wide = iota((reach, lanes), 1)
    for s in range(sources):
        at = pl.ds(s * slots, slots)
        product = sum(
            lax.dot_general(got_ref[2 * s + f], centres[f], last_last, preferred_element_type=f32)
            for f in range(2)
        )
        chosen = iota((slots, 8), 1).astype(f32) == column(turn_cols, s) - 1.0
        cosine = jnp.sum(jnp.where(chosen, product, 0.0), axis=1, keepdims=True) * inverse_ref[at, :]
        best = bests[s // group][(s % group) * slots : (s % group) * slots + reach]
        table = jnp.where(lane_wide == s, cosine[:reach], table)
        table = jnp.where(lane_wide == sources + s, best, table)
    if reach < lanes:
        table = jnp.concatenate([table, jnp.zeros((lanes - reach, lanes), f32)], axis=0)
    across = table.T
    row_bests = [row_best_ref[0:1, s * slots : s * slots + reach] for s in range(sources)]
    if reach < lanes:
        filler = jnp.full((1, lanes - reach), -1.0, f32)
        row_bests = [jnp.concatenate([part, filler], axis=1) for part in row_bests]
    cosine_parts = split3(across[:sources])
    best_parts = split3(jnp.maximum(across[sources : 2 * sources], jnp.concatenate(row_bests, axis=0)))
    row = iota((8, lanes), 0)
    for s in range(sources):
        answer = jnp.zeros((8, lanes), f32)
        for t, part in enumerate(cosine_parts + best_parts):
            answer = jnp.where(row == t, part[s : s + 1], answer)
        for f in range(2):
            back_ref[2 * s + f] = jnp.concatenate([centre_ref[f], answer], axis=1).astype(bf16)


def return_kernel(share, mine_ref, back_ref, info_ref, table_ref, centre_ref, cosine_ref, best_ref):
    dests = back_ref.shape[0]
    rows = info_ref.shape[1]
    step = 4 * lanes
    answers = back_ref[:, :, 256:].reshape(dests * 8, lanes)
    for b in range(rows // step):
        at = pl.ds(b * step, step)
        dest = info_ref[0:1, at]
        position = info_ref[1:2, at]
        place = jnp.where(iota((lanes, step), 0) == position, 1.0, 0.0).astype(bf16)
        picked = jnp.dot(answers, place, preferred_element_type=f32)
        picked = jnp.where(iota((dests * 8, step), 0) // 8 == dest, picked, 0.0)
        picked = jnp.sum(picked.reshape(dests, 8, step), axis=0)
        cosine = picked[0:1] + picked[1:2] + picked[2:3]
        best = picked[3:4] + picked[4:5] + picked[5:6]
        for c in range(step // lanes):
            row = b * (step // lanes) + c
            cosine_ref[row : row + 1, :] = cosine[:, c * lanes : (c + 1) * lanes]
            best_ref[row : row + 1, :] = best[:, c * lanes : (c + 1) * lanes]
    owned = centre_ref.shape[0]
    code = table_ref[pl.ds(pl.multiple_of(mine_ref[0] * owned, 8), owned), :][:, :1]
    dest = code // share
    turn = code - dest * share
    stored = back_ref[:, :, :256].reshape(dests * 8, 256)
    for h in range(2):
        want = dest * 8 + 2 * turn + h
        hits = jnp.where(iota((owned, dests * 8), 1) == want, 1.0, 0.0).astype(bf16)
        centre_ref[:, h * 256 : (h + 1) * 256] = jnp.dot(
            hits, stored, preferred_element_type=f32
        ).astype(bf16)


def vmem(count):
    return [pl.BlockSpec(memory_space=pltpu.VMEM)] * count


params = pltpu.CompilerParams(vmem_limit_bytes=50 * 1024 * 1024)


def exchange(x):
    return lax.all_to_all(x, AXES, split_axis=0, concat_axis=0, tiled=True)


def route(slots, embeddings, assignments, order_index, cluster_blocks):
    n_dp = lax.axis_size("dp")
    dests = n_dp * lax.axis_size("feat")
    rows, width = embeddings.shape
    clusters = cluster_blocks.shape[0]
    share = clusters // dests
    total = n_dp * slots

    sent, info, table = pl.pallas_call(
        partial(pack_kernel, dests, slots),
        out_shape=(
            jax.ShapeDtypeStruct((dests, slots, width), bf16),
            jax.ShapeDtypeStruct((8, rows), jnp.int32),
            jax.ShapeDtypeStruct((clusters, lanes), jnp.int32),
        ),
        in_specs=vmem(3) + [pl.BlockSpec(memory_space=pl.ANY)],
        out_specs=tuple(vmem(3)),
        scratch_shapes=[
            pltpu.VMEM((rows, width), bf16),
            pltpu.VMEM((4 * dests, rows), bf16),
            pltpu.VMEM((max(lanes, slots), rows), bf16),
            pltpu.VMEM((dests, rows), f32),
            pltpu.VMEM((dests * band, width), f32),
            pltpu.SemaphoreType.DMA,
        ],
        compiler_params=params,
        name="pack",
    )(
        assignments.reshape(rows // lanes, lanes),
        order_index.reshape(rows // lanes, lanes),
        cluster_blocks.reshape(1, clusters),
        embeddings,
    )
    got = exchange(sent)
    back, flag = pl.pallas_call(
        owner_kernel,
        out_shape=(
            jax.ShapeDtypeStruct((dests, 8, 384), bf16),
            jax.ShapeDtypeStruct((8, lanes), jnp.int32),
        ),
        in_specs=vmem(1),
        out_specs=tuple(vmem(2)),
        scratch_shapes=[
            pltpu.VMEM((total, 2 * width), bf16),
            pltpu.VMEM((total, 1), f32),
            pltpu.VMEM((lanes, lanes), f32),
            pltpu.VMEM((lanes, lanes), f32),
            pltpu.VMEM((1, total), f32),
            pltpu.VMEM((1, total), f32),
            pltpu.VMEM((1, total), f32),
            pltpu.VMEM((2, 8, 256), f32),
        ],
        compiler_params=params,
        name="owner",
    )(got)
    returned = exchange(back)
    mine = lax.axis_index("dp").reshape(1).astype(jnp.int32)
    centres, cosine, best = pl.pallas_call(
        partial(return_kernel, share),
        out_shape=(
            jax.ShapeDtypeStruct((clusters // n_dp, width), bf16),
            jax.ShapeDtypeStruct((rows // lanes, lanes), f32),
            jax.ShapeDtypeStruct((rows // lanes, lanes), f32),
        ),
        in_specs=[pl.BlockSpec(memory_space=pltpu.SMEM)] + vmem(3),
        out_specs=tuple(vmem(3)),
        compiler_params=params,
        name="answers",
    )(mine, returned, info, table)
    return (centres, cosine.reshape(rows), best.reshape(rows)), flag[0, 0] > 0


def body(embeddings, assignments, order_index, cluster_blocks):
    dests = lax.axis_size("dp") * lax.axis_size("feat")
    rows = assignments.shape[0]
    clusters = cluster_blocks.shape[0]
    most = (clusters // dests) * (2 * rows // clusters)
    args = (embeddings, assignments, order_index, cluster_blocks)
    few = -(-3 * most // (4 * band)) * band
    outputs, over = route(few, *args)
    return lax.cond(over, lambda: route(most + band, *args)[0], lambda: outputs)


def solution(mesh):
    return jax.shard_map(
        body,
        mesh=mesh,
        in_specs=(P("dp", "feat"), P("dp"), P("dp"), P()),
        out_specs=(P("dp", "feat"), P("dp"), P("dp")),
        check_vma=False,
    )
```

time: 116 us -> 111 us (0.957)
  Pallas kernels: 23.2 us -> 18.8 us
    pallas_call x1, Pallas kernels: 12.5 us -> 7.62 us  [route(): pl.pallas_call(owner_kernel, out_shape=(jax.ShapeDtypeStruct((dests, 8, 3...]
where the time goes in v2:
time: 111 us
  blocking collectives  77.6 us (70%)
  Pallas kernels  18.8 us (17%)
  waiting for transfers between devices  8.49 us (8%)
  starting transfers between devices  3.65 us (3%)
  between operations  1.5 us (1%)
    all_to_all x1, blocking collectives, exchange(): return lax.all_to_all(x, AXES, split_axis=0, concat_axis=0, tiled=True)  77.6 us
    pallas_call x1, Pallas kernels, route(): pl.pallas_call(partial(pack_kernel, dests, slots), out_shape=(jax.ShapeDt...  10.2 us
    all_to_all x1, waiting for transfers between devices, exchange(): return lax.all_to_all(x, AXES, split_axis=0, concat_axis=0, tiled=True)  8.49 us
    pallas_call x1, Pallas kernels, route(): pl.pallas_call(owner_kernel, out_shape=(jax.ShapeDtypeStruct((dests, 8, 3...  7.62 us
    all_to_all x1, starting transfers between devices, exchange(): return lax.all_to_all(x, AXES, split_axis=0, concat_axis=0, tiled=True)  3.65 us
  transfers between devices with their start and end apart: 1, of which 1 were waited for; matrix products, arithmetic and copies ran while one was open for 0% of the time, Pallas kernels for 0%

profile of v2, /device:TPU:0, one launch (start us, length us, event | category | flops | bytes accessed | tf_op | source)
XLA Modules:
  0.0 110.8 jit_solution(6947352998500688295)
XLA Ops:
  0.6 10.2 %pack.3 = (bf16[32,96,512]{2,1,0:T(8,128)(2,1)S(1)}, s32[8,2048]{1,0:T(8,128)S(1)}, s32[128,128]{1,0:T(8,128)S(1)}) custom-call(s32[16,128]{1,0:T(8,128)} %bitcast.11, s32[16,128]{1,0:T(8,128)} %bitcast.13, s32[1,128]{1,0:T(1,128)} %bitcast.15, bf16[2048,512]{1,0:T(8,128)(2,1)} %rows_hbm.1), custom_call_target="tpu_custom_call" | custom-call | tf_op jit(solution)/shard_map/pack/pallas_call | solution.py:283
  10.8 77.6 %all_to_all.19.got_ref = bf16[32,96,512]{2,1,0:T(8,128)(2,1)S(1)} all-to-all(bf16[32,96,512]{2,1,0:T(8,128)(2,1)S(1)} %get-tuple-element.44), channel_id=1, replica_groups=mesh['dp'=16,'feat'=2] {'dp','feat'}, dimensions={0} | all-to-all | bytes 6291456 | tf_op jit(solution)/shard_map/all_to_all | solution.py:272
  88.4 0.0 copy-start
  88.4 0.0 copy-start.1
  88.4 0.0 copy-start.2
  88.4 0.0 copy-start.3
  88.4 7.6 %owner.3 = (bf16[32,8,384]{2,1,0:T(8,128)(2,1)}, s32[8,128]{1,0:T(8,128)S(1)}) custom-call(bf16[32,96,512]{2,1,0:T(8,128)(2,1)S(1)} %all_to_all.19.got_ref), custom_call_target="tpu_custom_call" | custom-call | tf_op jit(solution)/shard_map/owner/pallas_call | solution.py:309
  96.0 3.6 %all-to-all-start.3 = ((bf16[32,8,384]{2,1,0:T(8,128)(2,1)}), bf16[32,8,384]{2,1,0:T(8,128)(2,1)S(1)}, u32[]{:S(2)}, u32[]{:S(2)}) async-start(bf16[32,8,384]{2,1,0:T(8,128)(2,1)} %get-tuple-element.46), calls=%async_computation.3 | async-start | bytes 393216 | tf_op jit(solution)/shard_map/all_to_all | solution.py:272
  99.7 0.5 slice.3
  100.8 8.5 %all-to-all-done.3.back_ref = bf16[32,8,384]{2,1,0:T(8,128)(2,1)S(1)} async-done(((bf16[32,8,384]{2,1,0:T(8,128)(2,1)}), bf16[32,8,384]{2,1,0:T(8,128)(2,1)S(1)}, u32[]{:S(2)}, u32[]{:S(2)}) %all-to-all-start.3) | async-done | bytes 196640 | tf_op jit(solution)/shard_map/all_to_all | solution.py:272
  109.3 1.1 answers.3
  110.4 0.0 copy-done
  110.4 0.0 copy-done.1
  110.4 0.0 copy-done.2
  110.4 0.0 copy-done.3
  110.4 0.2 conditional.1
Async XLA Ops:
  88.4 22.0 %copy-start = (bf16[2048,512]{1,0:T(8,128)(2,1)S(1)}, bf16[2048,512]{1,0:T(8,128)(2,1)}, u32[]{:S(2)}) copy-start(bf16[2048,512]{1,0:T(8,128)(2,1)} %rows_hbm.1) | copy-start | bytes 6291460
  88.4 22.0 %copy-start.1 = (s32[2048]{0:T(1024)S(1)}, s32[2048]{0:T(1024)}, u32[]{:S(2)}) copy-start(s32[2048]{0:T(1024)} %param.7) | copy-start | bytes 24580
  88.4 22.0 %copy-start.2 = (s32[2048]{0:T(1024)S(1)}, s32[2048]{0:T(1024)}, u32[]{:S(2)}) copy-start(s32[2048]{0:T(1024)} %param.8) | copy-start | bytes 24580
  88.4 22.0 %copy-start.3 = (s32[128]{0:T(128)S(1)}, s32[128]{0:T(128)}, u32[]{:S(2)}) copy-start(s32[128]{0:T(128)} %param.9) | copy-start | bytes 1540
  96.0 13.3 %all-to-all-start.3 = ((bf16[32,8,384]{2,1,0:T(8,128)(2,1)}), bf16[32,8,384]{2,1,0:T(8,128)(2,1)S(1)}, u32[]{:S(2)}, u32[]{:S(2)}) async-start(bf16[32,8,384]{2,1,0:T(8,128)(2,1)} %get-tuple-element.46), calls=%async_computation.3 | async-start | bytes 393216 | tf_op jit(solution)/shard_map/all_to_all | solution.py:272

commit v3 on v2

--- a/solution.py
+++ b/solution.py
@@ -21,27 +21,55 @@
     return lax.broadcasted_iota(jnp.int32, shape, dim)
 
 
+def deal_clusters(blocks, dests):
+    clusters = blocks.shape[1]
+    half = clusters // 2
+    square = (clusters, clusters)
+    here, there = iota(square, 0), iota(square, 1)
+    together = (here >= half) == (there >= half)
+
+    def counted(pairs, values=1.0):
+        return jnp.where(pairs, values, 0.0)
+
+    def down(table):
+        return jnp.sum(table, axis=0, keepdims=True)
+
+    def along(table):
+        return jnp.sum(table, axis=1, keepdims=True)
+
+    own_there = jnp.broadcast_to(blocks.astype(f32), square)
+    own_here = own_there.T
+    key_there = own_there * clusters + there.astype(f32)
+    key_here = own_here * clusters + here.astype(f32)
+    rank_here = along(counted(together & (key_there < key_here)))
+    rank_there = down(counted(together & (key_here < key_there)))
+    partner = together & (rank_here + rank_there == half - 1.0)
+
+    def pair_key(own, other, rank):
+        return (own + other) * clusters + jnp.minimum(rank, half - 1.0 - rank)
+
+    pair_here = pair_key(own_here[:, :1], along(counted(partner, own_there)), rank_here)
+    pair_there = pair_key(own_there[:1], down(counted(partner, own_here)), rank_there)
+    spot = along(counted(together & (pair_there < pair_here), 0.5))
+    is_upper = iota((clusters, 1), 0) >= half
+    spot = jnp.where(is_upper, dests - 1.0 - spot, spot)
+    turn = jnp.where(rank_here >= half // 2, 1.0, 0.0) + jnp.where(is_upper, 2.0, 0.0)
+    return spot * 4.0 + turn
+
+
 def pack_kernel(
     dests, slots, assign_ref, order_ref, blocks_ref, rows_hbm, out_ref, info_ref, table_ref,
-    rows_ref, pieces_ref, places_ref, hits_ref, total_ref, copy_sem,
+    rows_ref, pieces_ref, places_ref, hits_ref, copy_sem,
 ):
     clusters = blocks_ref.shape[1]
     rows, width = rows_ref.shape
-    share = clusters // dests
+    share = 4
     cap = slots - 1
     tall = places_ref.shape[0]
     copy = pltpu.make_async_copy(rows_hbm, rows_ref, copy_sem)
     copy.start()
 
-    sort_key = (blocks_ref[...] * clusters + iota((1, clusters), 1)).astype(f32)
-    key_cols = jnp.broadcast_to(sort_key, (clusters, clusters))
-    key_rows = key_cols.T
-    rank = jnp.sum(jnp.where(key_cols < key_rows, 1.0, 0.0), axis=1, keepdims=True)
-    turn = sum(jnp.where(rank >= t * dests, 1.0, 0.0) for t in range(1, share))
-    rest = rank - turn * dests
-    odd = (turn == 1.0) | (turn == 3.0)
-    dest_of = jnp.where(odd, dests - 1.0 - rest, rest)
-    code_of = dest_of * share + turn
+    code_of = deal_clusters(blocks_ref[...], dests)
     table_ref[...] = jnp.broadcast_to(code_of, table_ref.shape).astype(jnp.int32)
 
     step = 2 * lanes
@@ -85,21 +113,27 @@
     for p in range(0, slots, band):
         begin = sum(jnp.where(high <= p, 1, 0) for _, high in reach)
         end = sum(jnp.where(low < p + band, 1, 0) for low, _ in reach)
-        total_ref[...] = jnp.zeros_like(total_ref)
+        out_ref[:, p : p + band, :] = jnp.zeros((dests, band, width), bf16)
 
         def add(c, _):
             at = pl.ds(pl.multiple_of(c * chunk, chunk), chunk)
-            place = places_ref[p : p + band, at].astype(f32)
-            hits = hits_ref[:, at][:, None, :] * place[None, :, :]
-            hits = hits.reshape(dests * band, chunk).astype(bf16)
-            total_ref[...] += jnp.dot(hits, rows_ref[at, :], preferred_element_type=f32)
+            place = places_ref[p : p + band, at]
+            hits = jnp.concatenate(
+                [
+                    jnp.broadcast_to(hits_ref[d : d + 1, at], (16, chunk)).astype(bf16) * place[r : r + 16]
+                    for d in range(dests)
+                    for r in range(0, band, 16)
+                ],
+                axis=0,
+            )
+            placed = jnp.dot(hits, rows_ref[at, :], preferred_element_type=f32).astype(bf16)
+            out_ref[:, p : p + band, :] += placed.reshape(dests, band, width)
             return 0
 
         lax.fori_loop(begin, end, add, 0)
-        block = total_ref[...].reshape(dests, band, width)
-        if p + band == slots:
-            block = jnp.where(iota((dests, band, width), 1) == band - 1, note[:, None, :], block)
-        out_ref[:, p : p + band, :] = block.astype(bf16)
+    last = out_ref[:, slots - 16 :, :]
+    last = jnp.where(iota(last.shape, 1) == 15, note.astype(bf16)[:, None, :], last)
+    out_ref[:, slots - 16 :, :] = last
 
 
 def split3(value):
@@ -174,16 +208,17 @@
         turn_col = jnp.concatenate([column(turn_cols, s) for s in range(g * group, (g + 1) * group)], axis=0)
         order_col = jnp.concatenate([column(order_cols, s) for s in range(g * group, (g + 1) * group)], axis=0)
         units = unit_ref[mine, :]
-        best = jnp.full((span, 1), -1.0, f32)
-        for h in range(g + 1):
-            theirs = pl.ds(h * span, span)
-            similar = lax.dot_general(units, unit_ref[theirs, :], last_last, preferred_element_type=f32)
-            similar = jnp.where(turn_col == row_turn_ref[0:1, theirs], similar, -1.0)
-            earlier = row_order_ref[0:1, theirs] < order_col
-            best = jnp.maximum(best, jnp.max(jnp.where(earlier, similar, -1.0), axis=1, keepdims=True))
-            if h < g:
-                other = jnp.max(jnp.where(earlier, -1.0, similar), axis=0, keepdims=True)
-                row_best_ref[0:1, theirs] = jnp.maximum(row_best_ref[0:1, theirs], other)
+        near = pl.ds(0, (g + 1) * span)
+        similar = lax.dot_general(units, unit_ref[near, :], last_last, preferred_element_type=f32)
+        similar = jnp.where(turn_col == row_turn_ref[0:1, near], similar, -1.0)
+        earlier = row_order_ref[0:1, near] < order_col
+        best = jnp.max(jnp.where(earlier, similar, -1.0), axis=1, keepdims=True)
+        if g:
+            before = pl.ds(0, g * span)
+            later = jnp.where(earlier[:, : g * span], -1.0, similar[:, : g * span])
+            row_best_ref[0:1, before] = jnp.maximum(
+                row_best_ref[0:1, before], jnp.max(later, axis=0, keepdims=True)
+            )
         bests.append(best)
 
     counts = jnp.where(counts > 0.0, counts, 1.0)
@@ -193,32 +228,34 @@
     centres = [part / lengths for part in averages]
     for f in range(2):
         for j in range(4):
-            for h in range(2):
-                centre_ref[f, 2 * j + h : 2 * j + h + 1, :] = centres[f][j : j + 1, h * 256 : (h + 1) * 256]
+            for h in range(4):
+                row = 4 * (j % 2) + h
+                centre_ref[2 * (j // 2) + f, row : row + 1, :] = centres[f][j : j + 1, h * lanes : (h + 1) * lanes]
     centres = [part.astype(bf16) for part in centres]
 
-    cosines = jnp.zeros((reach, lanes), f32)
+    cosines = []
     table = jnp.zeros((reach, lanes), f32)
     lane_wide = iota((reach, lanes), 1)
     for s in range(sources):
-        at = pl.ds(s * slots, slots)
         product = sum(
-            lax.dot_general(got_ref[2 * s + f], centres[f], last_last, preferred_element_type=f32)
+            lax.dot_general(centres[f], got_ref[2 * s + f, :reach, :], last_last, preferred_element_type=f32)
             for f in range(2)
         )
-        chosen = iota((slots, 8), 1).astype(f32) == column(turn_cols, s) - 1.0
-        cosine = jnp.sum(jnp.where(chosen, product, 0.0), axis=1, keepdims=True) * inverse_ref[at, :]
+        chosen = iota((8, reach), 0).astype(f32) == turn_ref[s : s + 1, :reach] - 1.0
+        cosines.append(jnp.sum(jnp.where(chosen, product, 0.0), axis=0, keepdims=True))
+        inverse = inverse_ref[s * slots : s * slots + reach, :]
         best = bests[s // group][(s % group) * slots : (s % group) * slots + reach]
-        table = jnp.where(lane_wide == s, cosine[:reach], table)
+        table = jnp.where(lane_wide == s, inverse, table)
         table = jnp.where(lane_wide == sources + s, best, table)
     if reach < lanes:
         table = jnp.concatenate([table, jnp.zeros((lanes - reach, lanes), f32)], axis=0)
+        cosines = [jnp.concatenate([part, jnp.zeros((1, lanes - reach), f32)], axis=1) for part in cosines]
     across = table.T
     row_bests = [row_best_ref[0:1, s * slots : s * slots + reach] for s in range(sources)]
     if reach < lanes:
         filler = jnp.full((1, lanes - reach), -1.0, f32)
         row_bests = [jnp.concatenate([part, filler], axis=1) for part in row_bests]
-    cosine_parts = split3(across[:sources])
+    cosine_parts = split3(jnp.concatenate(cosines, axis=0) * across[:sources])
     best_parts = split3(jnp.maximum(across[sources : 2 * sources], jnp.concatenate(row_bests, axis=0)))
     row = iota((8, lanes), 0)
     for s in range(sources):
@@ -226,14 +263,14 @@
         for t, part in enumerate(cosine_parts + best_parts):
             answer = jnp.where(row == t, part[s : s + 1], answer)
         for f in range(2):
-            back_ref[2 * s + f] = jnp.concatenate([centre_ref[f], answer], axis=1).astype(bf16)
+            back_ref[2 * s + f] = jnp.concatenate([centre_ref[2 * (2 * s // sources) + f], answer], axis=1).astype(bf16)
 
 
 def return_kernel(share, mine_ref, back_ref, info_ref, table_ref, centre_ref, cosine_ref, best_ref):
     dests = back_ref.shape[0]
     rows = info_ref.shape[1]
     step = 4 * lanes
-    answers = back_ref[:, :, 256:].reshape(dests * 8, lanes)
+    answers = back_ref[:, :, lanes:].reshape(dests * 8, lanes)
     for b in range(rows // step):
         at = pl.ds(b * step, step)
         dest = info_ref[0:1, at]
@@ -252,11 +289,11 @@
     code = table_ref[pl.ds(pl.multiple_of(mine_ref[0] * owned, 8), owned), :][:, :1]
     dest = code // share
     turn = code - dest * share
-    stored = back_ref[:, :, :256].reshape(dests * 8, 256)
-    for h in range(2):
-        want = dest * 8 + 2 * turn + h
+    stored = back_ref[:, :, :lanes].reshape(dests * 8, lanes)
+    for h in range(4):
+        want = dest * 8 + 4 * (turn % 2) + h
         hits = jnp.where(iota((owned, dests * 8), 1) == want, 1.0, 0.0).astype(bf16)
-        centre_ref[:, h * 256 : (h + 1) * 256] = jnp.dot(
+        centre_ref[:, h * lanes : (h + 1) * lanes] = jnp.dot(
             hits, stored, preferred_element_type=f32
         ).astype(bf16)
 
@@ -294,7 +331,6 @@
             pltpu.VMEM((4 * dests, rows), bf16),
             pltpu.VMEM((max(lanes, slots), rows), bf16),
             pltpu.VMEM((dests, rows), f32),
-            pltpu.VMEM((dests * band, width), f32),
             pltpu.SemaphoreType.DMA,
         ],
         compiler_params=params,
@@ -309,7 +345,7 @@
     back, flag = pl.pallas_call(
         owner_kernel,
         out_shape=(
-            jax.ShapeDtypeStruct((dests, 8, 384), bf16),
+            jax.ShapeDtypeStruct((dests, 8, 2 * lanes), bf16),
             jax.ShapeDtypeStruct((8, lanes), jnp.int32),
         ),
         in_specs=vmem(1),
@@ -322,7 +358,7 @@
             pltpu.VMEM((1, total), f32),
             pltpu.VMEM((1, total), f32),
             pltpu.VMEM((1, total), f32),
-            pltpu.VMEM((2, 8, 256), f32),
+            pltpu.VMEM((4, 8, lanes), f32),
         ],
         compiler_params=params,
         name="owner",

time: 111 us -> 109 us (0.982)
  Pallas kernels: 18.8 us -> 16.8 us
  blocking collectives: 77.6 us -> 79 us
    pallas_call x1, Pallas kernels: 10.2 us -> 8.6 us  [route(): pl.pallas_call(partial(pack_kernel, dests, slots), out_shape=(jax.ShapeDt...]
    all_to_all x1, blocking collectives: 77.6 us -> 79 us  [exchange(): return lax.all_to_all(x, AXES, split_axis=0, concat_axis=0, tiled=True)]
where the time goes in v3:
time: 109 us
  blocking collectives  79 us (72%)
  Pallas kernels  16.8 us (15%)
  waiting for transfers between devices  7.45 us (7%)
  starting transfers between devices  3.65 us (3%)
  between operations  1.5 us (1%)
    all_to_all x1, blocking collectives, exchange(): return lax.all_to_all(x, AXES, split_axis=0, concat_axis=0, tiled=True)  79 us
    pallas_call x1, Pallas kernels, route(): pl.pallas_call(partial(pack_kernel, dests, slots), out_shape=(jax.ShapeDt...  8.6 us
    all_to_all x1, waiting for transfers between devices, exchange(): return lax.all_to_all(x, AXES, split_axis=0, concat_axis=0, tiled=True)  7.45 us
    pallas_call x1, Pallas kernels, route(): pl.pallas_call(owner_kernel, out_shape=(jax.ShapeDtypeStruct((dests, 8, 2...  7.09 us
    all_to_all x1, starting transfers between devices, exchange(): return lax.all_to_all(x, AXES, split_axis=0, concat_axis=0, tiled=True)  3.65 us
  transfers between devices with their start and end apart: 1, of which 1 were waited for; matrix products, arithmetic and copies ran while one was open for 0% of the time, Pallas kernels for 0%

profile of v3, /device:TPU:0, one launch (start us, length us, event | category | flops | bytes accessed | tf_op | source)
XLA Modules:
  0.0 109.2 jit_solution(10232893257405158939)
XLA Ops:
  0.6 8.6 %pack.3 = (bf16[32,96,512]{2,1,0:T(8,128)(2,1)S(1)}, s32[8,2048]{1,0:T(8,128)S(1)}, s32[128,128]{1,0:T(8,128)S(1)}) custom-call(s32[16,128]{1,0:T(8,128)} %bitcast.11, s32[16,128]{1,0:T(8,128)} %bitcast.13, s32[1,128]{1,0:T(1,128)} %bitcast.15, bf16[2048,512]{1,0:T(8,128)(2,1)} %rows_hbm.1), custom_call_target="tpu_custom_call" | custom-call | tf_op jit(solution)/shard_map/pack/pallas_call | solution.py:320
  9.2 79.0 %all_to_all.19.got_ref = bf16[32,96,512]{2,1,0:T(8,128)(2,1)S(1)} all-to-all(bf16[32,96,512]{2,1,0:T(8,128)(2,1)S(1)} %get-tuple-element.44), channel_id=1, replica_groups=mesh['dp'=16,'feat'=2] {'dp','feat'}, dimensions={0} | all-to-all | bytes 6291456 | tf_op jit(solution)/shard_map/all_to_all | solution.py:309
  88.2 0.0 copy-start
  88.2 0.0 copy-start.1
  88.2 0.0 copy-start.2
  88.3 0.0 copy-start.3
  88.3 7.1 %owner.3 = (bf16[32,8,256]{2,1,0:T(8,128)(2,1)}, s32[8,128]{1,0:T(8,128)S(1)}) custom-call(bf16[32,96,512]{2,1,0:T(8,128)(2,1)S(1)} %all_to_all.19.got_ref), custom_call_target="tpu_custom_call" | custom-call | tf_op jit(solution)/shard_map/owner/pallas_call | solution.py:345
  95.4 3.7 %all-to-all-start.3 = ((bf16[32,8,256]{2,1,0:T(8,128)(2,1)}), bf16[32,8,256]{2,1,0:T(8,128)(2,1)S(1)}, u32[]{:S(2)}, u32[]{:S(2)}) async-start(bf16[32,8,256]{2,1,0:T(8,128)(2,1)} %get-tuple-element.46), calls=%async_computation.3 | async-start | bytes 262144 | tf_op jit(solution)/shard_map/all_to_all | solution.py:309
  99.0 0.5 slice.3
  100.2 7.5 %all-to-all-done.3.back_ref = bf16[32,8,256]{2,1,0:T(8,128)(2,1)S(1)} async-done(((bf16[32,8,256]{2,1,0:T(8,128)(2,1)}), bf16[32,8,256]{2,1,0:T(8,128)(2,1)S(1)}, u32[]{:S(2)}, u32[]{:S(2)}) %all-to-all-start.3) | async-done | bytes 131104 | tf_op jit(solution)/shard_map/all_to_all | solution.py:309
  107.6 1.1 %answers.3 = (bf16[8,512]{1,0:T(8,128)(2,1)}, f32[16,128]{1,0:T(8,128)}, f32[16,128]{1,0:T(8,128)}) custom-call(s32[1]{0:T(128)} %bitcast.8.mine_ref, bf16[32,8,256]{2,1,0:T(8,128)(2,1)S(1)} %all-to-all-done.3.back_ref, s32[8,2048]{1,0:T(8,128)S(1)} %get-tuple-element.47.info_ref, s32[128,128]{1,0:T(8,128)S(1)} %get-tuple-element.48.table_ref), custom_call_target="tpu_custom_call" | custom-call | tf_op jit(solution)/shard_map/answers/pallas_call | solution.py:368
  108.7 0.0 copy-done
  108.7 0.0 copy-done.1
  108.7 0.0 copy-done.2
  108.7 0.0 copy-done.3
  108.8 0.2 conditional.1
Async XLA Ops:
  88.2 20.5 %copy-start = (bf16[2048,512]{1,0:T(8,128)(2,1)S(1)}, bf16[2048,512]{1,0:T(8,128)(2,1)}, u32[]{:S(2)}) copy-start(bf16[2048,512]{1,0:T(8,128)(2,1)} %rows_hbm.1) | copy-start | bytes 6291460
  88.2 20.5 %copy-start.1 = (s32[2048]{0:T(1024)S(1)}, s32[2048]{0:T(1024)}, u32[]{:S(2)}) copy-start(s32[2048]{0:T(1024)} %param.7) | copy-start | bytes 24580
  88.2 20.5 %copy-start.2 = (s32[2048]{0:T(1024)S(1)}, s32[2048]{0:T(1024)}, u32[]{:S(2)}) copy-start(s32[2048]{0:T(1024)} %param.8) | copy-start | bytes 24580
  88.3 20.5 %copy-start.3 = (s32[128]{0:T(128)S(1)}, s32[128]{0:T(128)}, u32[]{:S(2)}) copy-start(s32[128]{0:T(128)} %param.9) | copy-start | bytes 1540
  95.4 12.3 %all-to-all-start.3 = ((bf16[32,8,256]{2,1,0:T(8,128)(2,1)}), bf16[32,8,256]{2,1,0:T(8,128)(2,1)S(1)}, u32[]{:S(2)}, u32[]{:S(2)}) async-start(bf16[32,8,256]{2,1,0:T(8,128)(2,1)} %get-tuple-element.46), calls=%async_computation.3 | async-start | bytes 262144 | tf_op jit(solution)/shard_map/all_to_all | solution.py:309

commit v4 on v3

--- a/solution.py
+++ b/solution.py
@@ -58,14 +58,13 @@
 
 
 def pack_kernel(
-    dests, slots, assign_ref, order_ref, blocks_ref, rows_hbm, out_ref, info_ref, table_ref,
-    rows_ref, pieces_ref, places_ref, hits_ref, copy_sem,
+    dests, slots, spare, assign_ref, order_ref, blocks_ref, rows_hbm, out_ref, info_ref, table_ref,
+    rows_ref, pieces_ref, noted_ref, places_ref, hits_ref, copy_sem,
 ):
     clusters = blocks_ref.shape[1]
     rows, width = rows_ref.shape
     share = 4
     cap = slots - 1
-    tall = places_ref.shape[0]
     copy = pltpu.make_async_copy(rows_hbm, rows_ref, copy_sem)
     copy.start()
 
@@ -73,67 +72,94 @@
     table_ref[...] = jnp.broadcast_to(code_of, table_ref.shape).astype(jnp.int32)
 
     step = 2 * lanes
-    before = (iota((step, step), 0) < iota((step, step), 1)).astype(f32).astype(bf16)
+    steps = rows // step
+    before = jnp.where(iota((step, step), 0) < iota((step, step), 1), 1.0, 0.0).astype(bf16)
+
+    def row(ref, b):
+        return jnp.concatenate([ref[2 * b : 2 * b + 1], ref[2 * b + 1 : 2 * b + 2]], axis=1)
+
+    codes, hits = [], []
+    for b in range(steps):
+        member = iota((clusters, step), 0) == row(assign_ref, b)
+        code = jnp.sum(jnp.where(member, code_of, 0.0), axis=0, keepdims=True).astype(jnp.int32)
+        codes.append(code)
+        hits.append(jnp.where(iota((dests, step), 0) == code // 4, 1.0, 0.0))
+    stacked = jnp.concatenate(hits, axis=0)
+    ahead = jnp.dot(stacked.astype(bf16), before, preferred_element_type=f32)
+    held = jnp.sum(stacked, axis=1, keepdims=True)
     taken = jnp.zeros((dests, 1), f32)
     reach = []
-    for b in range(rows // step):
+    for b in range(steps):
         at = pl.ds(b * step, step)
-        assign = jnp.concatenate([assign_ref[2 * b : 2 * b + 1], assign_ref[2 * b + 1 : 2 * b + 2]], axis=1)
-        order = jnp.concatenate([order_ref[2 * b : 2 * b + 1], order_ref[2 * b + 1 : 2 * b + 2]], axis=1)
-        member = iota((clusters, step), 0) == assign
-        code = jnp.sum(jnp.where(member, code_of, 0.0), axis=0, keepdims=True).astype(jnp.int32)
-        dest = code // share
-        turn_row = code - dest * share
-        hit = iota((dests, step), 0) == dest
-        hit_f = jnp.where(hit, 1.0, 0.0)
-        hits_ref[:, at] = hit_f
-        ahead = jnp.dot(hit_f.astype(bf16), before, preferred_element_type=f32) + taken
+        mine = slice(b * dests, (b + 1) * dests)
         if b * step % chunk == 0:
             low = jnp.min(taken)
-        taken = taken + jnp.sum(hit_f, axis=1, keepdims=True)
+        place = jnp.sum(hits[b] * (ahead[mine] + taken), axis=0, keepdims=True)
+        taken = taken + held[mine]
         if (b + 1) * step % chunk == 0:
             reach.append((low, jnp.max(taken)))
-        position = jnp.sum(jnp.where(hit, ahead, 0.0), axis=0, keepdims=True).astype(jnp.int32)
+        dest = codes[b] // 4
+        position = place.astype(jnp.int32)
         info_ref[0:1, at] = dest
         info_ref[1:2, at] = position
-        fits = position < cap
-        parts = (order & 127, (order >> 7) & 127, order >> 14, turn_row + 1)
+        if spare:
+            over = position >= cap
+            target = jnp.where(over, dest ^ 2, dest)
+            there = jnp.where(over, jnp.where(position < cap + spare, position - spare, -1), position)
+            hits_ref[:, at] = jnp.where(iota((dests, step), 0) == target, 1.0, 0.0)
+        else:
+            there = jnp.where(position < cap, position, -1)
+            hits_ref[:, at] = hits[b]
+        order = row(order_ref, b)
+        parts = (order & 127, (order >> 7) & 127, order >> 14, codes[b] - dest * 4 + 1)
         for q, part in enumerate(parts):
-            pieces_ref[q * dests : (q + 1) * dests, at] = jnp.where(hit, part.astype(f32), 0.0).astype(bf16)
-        places_ref[:, at] = jnp.where((iota((tall, step), 0) == position) & fits, 1.0, 0.0).astype(bf16)
-
-    meta = lax.dot_general(pieces_ref[...], places_ref[:lanes, :], last_last, preferred_element_type=f32)
-    if cap < lanes:
-        most = jnp.max(taken, axis=0, keepdims=True)
+            pieces_ref[q * dests : (q + 1) * dests, at] = (hits[b] * part.astype(f32)).astype(bf16)
+        noted_ref[:, at] = jnp.where(iota((lanes, step), 0) == position, 1.0, 0.0).astype(bf16)
+        places_ref[:, at] = jnp.where(iota((places_ref.shape[0], step), 0) == there, 1.0, 0.0).astype(bf16)
+
+    meta = lax.dot_general(pieces_ref[...], noted_ref[...], last_last, preferred_element_type=f32)
+    if spare:
+        square = (dests, dests)
+        loads = jnp.broadcast_to(taken, square).T
+        sibling = jnp.sum(
+            jnp.where(iota(square, 1) == (iota(square, 0) ^ 2), loads, 0.0), axis=1, keepdims=True
+        )
+        over = taken > cap
+        stuck = over & ((taken > cap + spare) | (sibling > cap - spare))
+        level = jnp.where(over, 1.0, 0.0) + jnp.where(stuck, 1.0, 0.0)
+        level = jnp.max(level, axis=0, keepdims=True)
         flagged = (iota(meta.shape, 0) >= 3 * dests) & (iota(meta.shape, 1) == lanes - 1)
-        meta = jnp.where(flagged, most, meta)
+        meta = jnp.where(flagged, level, meta)
     copy.wait()
 
     note = jnp.concatenate([meta[q * dests : (q + 1) * dests] for q in range(4)], axis=1)
     for p in range(0, slots, band):
+        tall = min(band, slots - p)
         begin = sum(jnp.where(high <= p, 1, 0) for _, high in reach)
-        end = sum(jnp.where(low < p + band, 1, 0) for low, _ in reach)
-        out_ref[:, p : p + band, :] = jnp.zeros((dests, band, width), bf16)
+        end = sum(jnp.where(low < p + tall, 1, 0) for low, _ in reach)
+        out_ref[:, p : p + tall, :] = jnp.zeros((dests, tall, width), bf16)
 
         def add(c, _):
             at = pl.ds(pl.multiple_of(c * chunk, chunk), chunk)
-            place = places_ref[p : p + band, at]
+            place = places_ref[p : p + tall, at]
             hits = jnp.concatenate(
                 [
-                    jnp.broadcast_to(hits_ref[d : d + 1, at], (16, chunk)).astype(bf16) * place[r : r + 16]
+                    jnp.broadcast_to(hits_ref[d : d + 1, at], (min(16, tall - r), chunk)).astype(bf16)
+                    * place[r : r + 16]
                     for d in range(dests)
-                    for r in range(0, band, 16)
+                    for r in range(0, tall, 16)
                 ],
                 axis=0,
             )
             placed = jnp.dot(hits, rows_ref[at, :], preferred_element_type=f32).astype(bf16)
-            out_ref[:, p : p + band, :] += placed.reshape(dests, band, width)
+            out_ref[:, p : p + tall, :] += placed.reshape(dests, tall, width)
             return 0
 
         lax.fori_loop(begin, end, add, 0)
-    last = out_ref[:, slots - 16 :, :]
-    last = jnp.where(iota(last.shape, 1) == 15, note.astype(bf16)[:, None, :], last)
-    out_ref[:, slots - 16 :, :] = last
+    at = pl.ds(p, tall)
+    last = out_ref[:, at, :]
+    last = jnp.where(iota(last.shape, 1) == tall - 1, note.astype(bf16)[:, None, :], last)
+    out_ref[:, at, :] = last
 
 
 def split3(value):
@@ -142,14 +168,29 @@
     return high, middle, value - high - middle
 
 
-def owner_kernel(
-    got_ref, back_ref, flag_ref, unit_ref, inverse_ref, order_ref, turn_ref, row_order_ref, row_turn_ref, row_best_ref, centre_ref,
-):
-    blocks, slots, width = got_ref.shape
+def owner_kernel(spare, got_ref, *refs):
+    more_ref, refs = (refs[0], refs[1:]) if spare else (None, refs)
+    back_ref, flag_ref, unit_ref, inverse_ref, order_ref, turn_ref, *refs = refs
+    row_order_ref, row_turn_ref, row_best_ref, centre_ref = refs
+    blocks, sent, width = got_ref.shape
     sources = blocks // 2
-    cap = slots - 1
+    cap = sent - 1
+    slots = sent + 16 if spare else sent
+    shift = 16 - spare
     reach = min(slots, lanes)
     lane = iota((1, lanes), 1)
+    moved = (lane >= cap + shift) & (lane < cap + shift + spare)
+
+    def block(s, f):
+        if spare:
+            both = got_ref[2 * s + f].astype(f32), more_ref[2 * s + f].astype(f32)
+            return jnp.concatenate(both, axis=0).astype(bf16)
+        return got_ref[2 * s + f]
+
+    def by_slot(values):
+        kept = jnp.where(lane < cap, values, 0.0)
+        return jnp.where(moved, pltpu.roll(values, shift, 1), kept) if spare else kept
+
     most = jnp.zeros((1, 1), f32)
 
     order_ref[...] = jnp.zeros_like(order_ref)
@@ -159,16 +200,18 @@
         row_turn_ref[...] = jnp.zeros_like(row_turn_ref)
         row_order_ref[...] = jnp.zeros_like(row_order_ref)
     for s in range(sources):
-        note = got_ref[2 * s, slots - band : slots, :].astype(f32)[band - 1 :]
-        turn = jnp.where(lane < cap, note[:, 3 * lanes : 4 * lanes], 0.0)
-        order = note[:, :lanes] + 128.0 * note[:, lanes : 2 * lanes] + 16384.0 * note[:, 2 * lanes : 3 * lanes]
+        note = got_ref[2 * s, cap // 16 * 16 :, :].astype(f32)[cap % 16 :]
+        turn = by_slot(note[:, 3 * lanes : 4 * lanes])
+        order = by_slot(
+            note[:, :lanes] + 128.0 * note[:, lanes : 2 * lanes] + 16384.0 * note[:, 2 * lanes : 3 * lanes]
+        )
         if cap < lanes:
             most = jnp.maximum(most, note[:, 4 * lanes - 1 : 4 * lanes])
         turn_ref[s : s + 1, :] = turn
         order_ref[s : s + 1, :] = order
         row_turn_ref[0:1, s * slots : s * slots + reach] = turn[:, :reach]
         row_order_ref[0:1, s * slots : s * slots + reach] = order[:, :reach]
-    flag_ref[...] = jnp.broadcast_to(jnp.where(most > cap, 1, 0), flag_ref.shape).astype(jnp.int32)
+    flag_ref[...] = jnp.broadcast_to(most, flag_ref.shape).astype(jnp.int32)
     order_cols = order_ref[...].T
     turn_cols = turn_ref[...].T
 
@@ -178,19 +221,20 @@
             col = jnp.concatenate([col, jnp.zeros((slots - reach, 1), f32)], axis=0)
         return col
 
-    group = max(1, 384 // slots)
+    group = max(1, 416 // slots)
     while sources % group:
         group -= 1
     span = group * slots
     sums = [jnp.zeros((8, width), f32) for _ in range(2)]
     counts = jnp.zeros((8, 1), f32)
-    bests = []
+    bests, cosines = [], []
     for g in range(sources // group):
         mine = pl.ds(g * span, span)
         for s in range(g * group, (g + 1) * group):
             at = pl.ds(s * slots, slots)
-            first = got_ref[2 * s].astype(f32)
-            second = got_ref[2 * s + 1].astype(f32)
+            raw = block(s, 0), block(s, 1)
+            first = raw[0].astype(f32)
+            second = raw[1].astype(f32)
             squares = jnp.sum(first * first + second * second, axis=1, keepdims=True)
             inverse = 1.0 / jnp.sqrt(squares + epsilon)
             inverse_ref[at, :] = inverse
@@ -203,10 +247,30 @@
             member = member.astype(bf16)
             for f in range(2):
                 sums[f] = sums[f] + jnp.dot(
-                    member, got_ref[2 * s + f, :reach, :], preferred_element_type=f32
+                    member, raw[f][:reach], preferred_element_type=f32
                 )
         turn_col = jnp.concatenate([column(turn_cols, s) for s in range(g * group, (g + 1) * group)], axis=0)
         order_col = jnp.concatenate([column(order_cols, s) for s in range(g * group, (g + 1) * group)], axis=0)
+        if (g + 1) * group == sources:
+            counts = jnp.where(counts > 0.0, counts, 1.0)
+            averages = [part / counts for part in sums]
+            norms = jnp.sum(averages[0] * averages[0] + averages[1] * averages[1], axis=1, keepdims=True)
+            lengths = jnp.sqrt(norms + epsilon)
+            centres = [part / lengths for part in averages]
+            for f in range(2):
+                for j in range(4):
+                    for h in range(4):
+                        row = 4 * (j % 2) + h
+                        centre_ref[2 * (j // 2) + f, row : row + 1, :] = centres[f][j : j + 1, h * lanes : (h + 1) * lanes]
+            centres = [part.astype(bf16) for part in centres]
+
+            for s in range(sources):
+                product = sum(
+                    lax.dot_general(centres[f], block(s, f)[:reach], last_last, preferred_element_type=f32)
+                    for f in range(2)
+                )
+                chosen = iota((8, reach), 0).astype(f32) == turn_ref[s : s + 1, :reach] - 1.0
+                cosines.append(jnp.sum(jnp.where(chosen, product, 0.0), axis=0, keepdims=True))
         units = unit_ref[mine, :]
         near = pl.ds(0, (g + 1) * span)
         similar = lax.dot_general(units, unit_ref[near, :], last_last, preferred_element_type=f32)
@@ -221,28 +285,9 @@
             )
         bests.append(best)
 
-    counts = jnp.where(counts > 0.0, counts, 1.0)
-    averages = [part / counts for part in sums]
-    norms = jnp.sum(averages[0] * averages[0] + averages[1] * averages[1], axis=1, keepdims=True)
-    lengths = jnp.sqrt(norms + epsilon)
-    centres = [part / lengths for part in averages]
-    for f in range(2):
-        for j in range(4):
-            for h in range(4):
-                row = 4 * (j % 2) + h
-                centre_ref[2 * (j // 2) + f, row : row + 1, :] = centres[f][j : j + 1, h * lanes : (h + 1) * lanes]
-    centres = [part.astype(bf16) for part in centres]
-
-    cosines = []
     table = jnp.zeros((reach, lanes), f32)
     lane_wide = iota((reach, lanes), 1)
     for s in range(sources):
-        product = sum(
-            lax.dot_general(centres[f], got_ref[2 * s + f, :reach, :], last_last, preferred_element_type=f32)
-            for f in range(2)
-        )
-        chosen = iota((8, reach), 0).astype(f32) == turn_ref[s : s + 1, :reach] - 1.0
-        cosines.append(jnp.sum(jnp.where(chosen, product, 0.0), axis=0, keepdims=True))
         inverse = inverse_ref[s * slots : s * slots + reach, :]
         best = bests[s // group][(s % group) * slots : (s % group) * slots + reach]
         table = jnp.where(lane_wide == s, inverse, table)
@@ -255,8 +300,13 @@
     if reach < lanes:
         filler = jnp.full((1, lanes - reach), -1.0, f32)
         row_bests = [jnp.concatenate([part, filler], axis=1) for part in row_bests]
-    cosine_parts = split3(jnp.concatenate(cosines, axis=0) * across[:sources])
-    best_parts = split3(jnp.maximum(across[sources : 2 * sources], jnp.concatenate(row_bests, axis=0)))
+    cosine = jnp.concatenate(cosines, axis=0) * across[:sources]
+    best = jnp.maximum(across[sources : 2 * sources], jnp.concatenate(row_bests, axis=0))
+    if spare:
+        cosine = jnp.where(lane < cap, cosine, pltpu.roll(cosine, lanes - shift, 1))
+        best = jnp.where(lane < cap, best, pltpu.roll(best, lanes - shift, 1))
+    cosine_parts = split3(cosine)
+    best_parts = split3(best)
     row = iota((8, lanes), 0)
     for s in range(sources):
         answer = jnp.zeros((8, lanes), f32)
@@ -309,16 +359,12 @@
     return lax.all_to_all(x, AXES, split_axis=0, concat_axis=0, tiled=True)
 
 
-def route(slots, embeddings, assignments, order_index, cluster_blocks):
-    n_dp = lax.axis_size("dp")
-    dests = n_dp * lax.axis_size("feat")
+def send(slots, spare, embeddings, assignments, order_index, cluster_blocks):
+    dests = lax.axis_size("dp") * lax.axis_size("feat")
     rows, width = embeddings.shape
     clusters = cluster_blocks.shape[0]
-    share = clusters // dests
-    total = n_dp * slots
-
     sent, info, table = pl.pallas_call(
-        partial(pack_kernel, dests, slots),
+        partial(pack_kernel, dests, slots, spare),
         out_shape=(
             jax.ShapeDtypeStruct((dests, slots, width), bf16),
             jax.ShapeDtypeStruct((8, rows), jnp.int32),
@@ -329,7 +375,8 @@
         scratch_shapes=[
             pltpu.VMEM((rows, width), bf16),
             pltpu.VMEM((4 * dests, rows), bf16),
-            pltpu.VMEM((max(lanes, slots), rows), bf16),
+            pltpu.VMEM((lanes, rows), bf16),
+            pltpu.VMEM((-(-slots // 16) * 16, rows), bf16),
             pltpu.VMEM((dests, rows), f32),
             pltpu.SemaphoreType.DMA,
         ],
@@ -341,14 +388,21 @@
         cluster_blocks.reshape(1, clusters),
         embeddings,
     )
-    got = exchange(sent)
-    back, flag = pl.pallas_call(
-        owner_kernel,
+    return exchange(sent), info, table
+
+
+def answer(spare, got, info, table):
+    n_dp = lax.axis_size("dp")
+    dests, slots, width = got[0].shape
+    total = n_dp * sum(part.shape[1] for part in got)
+    rows = info.shape[1]
+    back, level = pl.pallas_call(
+        partial(owner_kernel, spare),
         out_shape=(
             jax.ShapeDtypeStruct((dests, 8, 2 * lanes), bf16),
             jax.ShapeDtypeStruct((8, lanes), jnp.int32),
         ),
-        in_specs=vmem(1),
+        in_specs=vmem(len(got)),
         out_specs=tuple(vmem(2)),
         scratch_shapes=[
             pltpu.VMEM((total, 2 * width), bf16),
@@ -362,13 +416,13 @@
         ],
         compiler_params=params,
         name="owner",
-    )(got)
+    )(*got)
     returned = exchange(back)
     mine = lax.axis_index("dp").reshape(1).astype(jnp.int32)
     centres, cosine, best = pl.pallas_call(
-        partial(return_kernel, share),
+        partial(return_kernel, 4),
         out_shape=(
-            jax.ShapeDtypeStruct((clusters // n_dp, width), bf16),
+            jax.ShapeDtypeStruct((table.shape[0] // n_dp, width), bf16),
             jax.ShapeDtypeStruct((rows // lanes, lanes), f32),
             jax.ShapeDtypeStruct((rows // lanes, lanes), f32),
         ),
@@ -377,18 +431,29 @@
         compiler_params=params,
         name="answers",
     )(mine, returned, info, table)
-    return (centres, cosine.reshape(rows), best.reshape(rows)), flag[0, 0] > 0
+    return (centres, cosine.reshape(rows), best.reshape(rows)), level[0, 0]
 
 
 def body(embeddings, assignments, order_index, cluster_blocks):
-    dests = lax.axis_size("dp") * lax.axis_size("feat")
+    n_dp = lax.axis_size("dp")
+    dests = n_dp * lax.axis_size("feat")
     rows = assignments.shape[0]
     clusters = cluster_blocks.shape[0]
     most = (clusters // dests) * (2 * rows // clusters)
     args = (embeddings, assignments, order_index, cluster_blocks)
-    few = -(-3 * most // (4 * band)) * band
-    outputs, over = route(few, *args)
-    return lax.cond(over, lambda: route(most + band, *args)[0], lambda: outputs)
+    few = -(-11 * most // 128) * 8
+    got, info, table = send(few, 8, *args)
+    outputs, level = answer(0, (got,), info, table)
+
+    def with_sibling():
+        more = lax.ppermute(got[:, few - 16 :], "dp", [(i, i ^ 1) for i in range(n_dp)])
+        return answer(8, (got, more), info, table)[0]
+
+    def with_all():
+        got, info, table = send(most + 32, 0, *args)
+        return answer(0, (got,), info, table)[0]
+
+    return lax.switch(level, [lambda: outputs, with_sibling, with_all])
 
 
 def solution(mesh):

time: 109 us -> 102 us (0.936)
  blocking collectives: 79 us -> 72.7 us
    all_to_all x1, blocking collectives: 79 us -> 72.7 us  [exchange(): return lax.all_to_all(x, AXES, split_axis=0, concat_axis=0, tiled=True)]
  transfers between devices with their start and end apart: 1 -> 1, of which waited for: 1 -> 1; matrix products, arithmetic and copies ran while one was open for 0% -> 1% of each run, Pallas kernels for 0% -> 0%
where the time goes in v4:
time: 102 us
  blocking collectives  72.7 us (71%)
  Pallas kernels  16.1 us (16%)
  waiting for transfers between devices  7.45 us (7%)
  starting transfers between devices  3.65 us (4%)
  between operations  1.49 us (1%)
    all_to_all x1, blocking collectives, exchange(): return lax.all_to_all(x, AXES, split_axis=0, concat_axis=0, tiled=True)  72.7 us
    pallas_call x1, Pallas kernels, send(): pl.pallas_call(partial(pack_kernel, dests, slots, spare), out_shape=(jax....  8.39 us
    all_to_all x1, waiting for transfers between devices, exchange(): return lax.all_to_all(x, AXES, split_axis=0, concat_axis=0, tiled=True)  7.45 us
    pallas_call x1, Pallas kernels, answer(): pl.pallas_call(partial(owner_kernel, spare), out_shape=(jax.ShapeDtypeStr...  6.56 us
    all_to_all x1, starting transfers between devices, exchange(): return lax.all_to_all(x, AXES, split_axis=0, concat_axis=0, tiled=True)  3.65 us
  transfers between devices with their start and end apart: 1, of which 1 were waited for; matrix products, arithmetic and copies ran while one was open for 1% of the time, Pallas kernels for 0%

profile of v4, /device:TPU:0, one launch (start us, length us, event | category | flops | bytes accessed | tf_op | source)
XLA Modules:
  0.0 102.1 jit_solution(18428744082261847701)
XLA Ops:
  0.6 8.4 %pack.3 = (bf16[32,88,512]{2,1,0:T(8,128)(2,1)S(1)}, s32[8,2048]{1,0:T(8,128)S(1)}, s32[128,128]{1,0:T(8,128)S(1)}) custom-call(s32[16,128]{1,0:T(8,128)} %bitcast.12, s32[16,128]{1,0:T(8,128)} %bitcast.14, s32[1,128]{1,0:T(1,128)} %bitcast.16, bf16[2048,512]{1,0:T(8,128)(2,1)} %rows_hbm.1), custom_call_target="tpu_custom_call" | custom-call | tf_op jit(solution)/shard_map/pack/pallas_call | solution.py:366
  9.0 72.7 %all_to_all.23.got_ref = bf16[32,88,512]{2,1,0:T(8,128)(2,1)S(1)} all-to-all(bf16[32,88,512]{2,1,0:T(8,128)(2,1)S(1)} %get-tuple-element.57), channel_id=1, replica_groups=mesh['dp'=16,'feat'=2] {'dp','feat'}, dimensions={0} | all-to-all | bytes 5767168 | tf_op jit(solution)/shard_map/all_to_all | solution.py:359
  81.7 0.0 copy-start
  81.7 0.0 copy-start.1
  81.7 0.0 copy-start.2
  81.7 6.6 %owner.5 = (bf16[32,8,256]{2,1,0:T(8,128)(2,1)}, s32[8,128]{1,0:T(8,128)S(1)}) custom-call(bf16[32,88,512]{2,1,0:T(8,128)(2,1)S(1)} %all_to_all.23.got_ref), custom_call_target="tpu_custom_call" | custom-call | tf_op jit(solution)/shard_map/owner/pallas_call | solution.py:399
  88.3 3.6 %all-to-all-start.4 = ((bf16[32,8,256]{2,1,0:T(8,128)(2,1)}), bf16[32,8,256]{2,1,0:T(8,128)(2,1)S(1)}, u32[]{:S(2)}, u32[]{:S(2)}) async-start(bf16[32,8,256]{2,1,0:T(8,128)(2,1)} %get-tuple-element.59), calls=%async_computation.4 | async-start | bytes 262144 | tf_op jit(solution)/shard_map/all_to_all | solution.py:359
  91.9 0.5 slice.6
  93.1 7.5 %all-to-all-done.4.back_ref = bf16[32,8,256]{2,1,0:T(8,128)(2,1)S(1)} async-done(((bf16[32,8,256]{2,1,0:T(8,128)(2,1)}), bf16[32,8,256]{2,1,0:T(8,128)(2,1)S(1)}, u32[]{:S(2)}, u32[]{:S(2)}) %all-to-all-start.4) | async-done | bytes 131104 | tf_op jit(solution)/shard_map/all_to_all | solution.py:359
  100.6 1.1 %answers.5 = (bf16[8,512]{1,0:T(8,128)(2,1)}, f32[16,128]{1,0:T(8,128)}, f32[16,128]{1,0:T(8,128)}) custom-call(s32[1]{0:T(128)} %bitcast.9.mine_ref, bf16[32,8,256]{2,1,0:T(8,128)(2,1)S(1)} %all-to-all-done.4.back_ref, s32[8,2048]{1,0:T(8,128)S(1)} %get-tuple-element.60.info_ref, s32[128,128]{1,0:T(8,128)S(1)} %get-tuple-element.61.table_ref), custom_call_target="tpu_custom_call" | custom-call | tf_op jit(solution)/shard_map/answers/pallas_call | solution.py:422
  101.7 0.0 copy-done
  101.7 0.0 copy-done.1
  101.7 0.0 copy-done.2
  101.7 0.2 conditional.1
Async XLA Ops:
  81.7 20.0 %copy-start = (s32[2048]{0:T(1024)S(1)}, s32[2048]{0:T(1024)}, u32[]{:S(2)}) copy-start(s32[2048]{0:T(1024)} %param.8) | copy-start | bytes 24580
  81.7 20.0 %copy-start.1 = (s32[2048]{0:T(1024)S(1)}, s32[2048]{0:T(1024)}, u32[]{:S(2)}) copy-start(s32[2048]{0:T(1024)} %param.9) | copy-start | bytes 24580
  81.7 20.0 %copy-start.2 = (s32[128]{0:T(128)S(1)}, s32[128]{0:T(128)}, u32[]{:S(2)}) copy-start(s32[128]{0:T(128)} %param.10) | copy-start | bytes 1540
  88.3 12.3 %all-to-all-start.4 = ((bf16[32,8,256]{2,1,0:T(8,128)(2,1)}), bf16[32,8,256]{2,1,0:T(8,128)(2,1)S(1)}, u32[]{:S(2)}, u32[]{:S(2)}) async-start(bf16[32,8,256]{2,1,0:T(8,128)(2,1)} %get-tuple-element.59), calls=%async_computation.4 | async-start | bytes 262144 | tf_op jit(solution)/shard_map/all_to_all | solution.py:359

commit v5 on v4

--- a/solution.py
+++ b/solution.py
@@ -230,25 +230,27 @@
     bests, cosines = [], []
     for g in range(sources // group):
         mine = pl.ds(g * span, span)
-        for s in range(g * group, (g + 1) * group):
-            at = pl.ds(s * slots, slots)
-            raw = block(s, 0), block(s, 1)
-            first = raw[0].astype(f32)
-            second = raw[1].astype(f32)
+        for s in range(g * group, (g + 1) * group, 2):
+            at = pl.ds(s * slots, 2 * slots)
+            raw = [[block(s + i, f) for f in range(2)] for i in range(2)]
+            first, second = [
+                jnp.concatenate([raw[0][f].astype(f32), raw[1][f].astype(f32)], axis=0) for f in range(2)
+            ]
             squares = jnp.sum(first * first + second * second, axis=1, keepdims=True)
             inverse = 1.0 / jnp.sqrt(squares + epsilon)
             inverse_ref[at, :] = inverse
             unit_ref[at, :width] = (first * inverse).astype(bf16)
             unit_ref[at, width:] = (second * inverse).astype(bf16)
-            member = jnp.where(
-                iota((8, reach), 0).astype(f32) == turn_ref[s : s + 1, :reach] - 1.0, 1.0, 0.0
-            )
-            counts = counts + jnp.sum(member, axis=1, keepdims=True)
-            member = member.astype(bf16)
-            for f in range(2):
-                sums[f] = sums[f] + jnp.dot(
-                    member, raw[f][:reach], preferred_element_type=f32
+            for i in range(2):
+                member = jnp.where(
+                    iota((8, reach), 0).astype(f32) == turn_ref[s + i : s + i + 1, :reach] - 1.0, 1.0, 0.0
                 )
+                counts = counts + jnp.sum(member, axis=1, keepdims=True)
+                member = member.astype(bf16)
+                for f in range(2):
+                    sums[f] = sums[f] + jnp.dot(
+                        member, raw[i][f][:reach], preferred_element_type=f32
+                    )
         turn_col = jnp.concatenate([column(turn_cols, s) for s in range(g * group, (g + 1) * group)], axis=0)
         order_col = jnp.concatenate([column(order_cols, s) for s in range(g * group, (g + 1) * group)], axis=0)
         if (g + 1) * group == sources:

time: 102 us -> 102 us (level)
  no operation moved by 1% of the time
where the time goes in v5:
time: 102 us
  blocking collectives  72.8 us (71%)
  Pallas kernels  16 us (16%)
  waiting for transfers between devices  7.45 us (7%)
  starting transfers between devices  3.65 us (4%)
  between operations  1.49 us (1%)
    all_to_all x1, blocking collectives, exchange(): return lax.all_to_all(x, AXES, split_axis=0, concat_axis=0, tiled=True)  72.8 us
    pallas_call x1, Pallas kernels, send(): pl.pallas_call(partial(pack_kernel, dests, slots, spare), out_shape=(jax....  8.39 us
    all_to_all x1, waiting for transfers between devices, exchange(): return lax.all_to_all(x, AXES, split_axis=0, concat_axis=0, tiled=True)  7.45 us
    pallas_call x1, Pallas kernels, answer(): pl.pallas_call(partial(owner_kernel, spare), out_shape=(jax.ShapeDtypeStr...  6.56 us
    all_to_all x1, starting transfers between devices, exchange(): return lax.all_to_all(x, AXES, split_axis=0, concat_axis=0, tiled=True)  3.65 us
  transfers between devices with their start and end apart: 1, of which 1 were waited for; matrix products, arithmetic and copies ran while one was open for 1% of the time, Pallas kernels for 0%

profile of v5, /device:TPU:0, one launch (start us, length us, event | category | flops | bytes accessed | tf_op | source)
XLA Modules:
  0.0 102.2 jit_solution(18428744082261847701)
XLA Ops:
  0.6 8.4 %pack.3 = (bf16[32,88,512]{2,1,0:T(8,128)(2,1)S(1)}, s32[8,2048]{1,0:T(8,128)S(1)}, s32[128,128]{1,0:T(8,128)S(1)}) custom-call(s32[16,128]{1,0:T(8,128)} %bitcast.12, s32[16,128]{1,0:T(8,128)} %bitcast.14, s32[1,128]{1,0:T(1,128)} %bitcast.16, bf16[2048,512]{1,0:T(8,128)(2,1)} %rows_hbm.1), custom_call_target="tpu_custom_call" | custom-call | tf_op jit(solution)/shard_map/pack/pallas_call | solution.py:368
  9.0 72.8 %all_to_all.23.got_ref = bf16[32,88,512]{2,1,0:T(8,128)(2,1)S(1)} all-to-all(bf16[32,88,512]{2,1,0:T(8,128)(2,1)S(1)} %get-tuple-element.57), channel_id=1, replica_groups=mesh['dp'=16,'feat'=2] {'dp','feat'}, dimensions={0} | all-to-all | bytes 5767168 | tf_op jit(solution)/shard_map/all_to_all | solution.py:361
  81.9 0.0 copy-start
  81.9 0.0 copy-start.1
  81.9 0.0 copy-start.2
  81.9 6.6 %owner.5 = (bf16[32,8,256]{2,1,0:T(8,128)(2,1)}, s32[8,128]{1,0:T(8,128)S(1)}) custom-call(bf16[32,88,512]{2,1,0:T(8,128)(2,1)S(1)} %all_to_all.23.got_ref), custom_call_target="tpu_custom_call" | custom-call | tf_op jit(solution)/shard_map/owner/pallas_call | solution.py:401
  88.4 3.6 %all-to-all-start.4 = ((bf16[32,8,256]{2,1,0:T(8,128)(2,1)}), bf16[32,8,256]{2,1,0:T(8,128)(2,1)S(1)}, u32[]{:S(2)}, u32[]{:S(2)}) async-start(bf16[32,8,256]{2,1,0:T(8,128)(2,1)} %get-tuple-element.59), calls=%async_computation.4 | async-start | bytes 262144 | tf_op jit(solution)/shard_map/all_to_all | solution.py:361
  92.1 0.5 slice.6
  93.3 7.5 %all-to-all-done.4.back_ref = bf16[32,8,256]{2,1,0:T(8,128)(2,1)S(1)} async-done(((bf16[32,8,256]{2,1,0:T(8,128)(2,1)}), bf16[32,8,256]{2,1,0:T(8,128)(2,1)S(1)}, u32[]{:S(2)}, u32[]{:S(2)}) %all-to-all-start.4) | async-done | bytes 131104 | tf_op jit(solution)/shard_map/all_to_all | solution.py:361
  100.7 1.1 %answers.5 = (bf16[8,512]{1,0:T(8,128)(2,1)}, f32[16,128]{1,0:T(8,128)}, f32[16,128]{1,0:T(8,128)}) custom-call(s32[1]{0:T(128)} %bitcast.9.mine_ref, bf16[32,8,256]{2,1,0:T(8,128)(2,1)S(1)} %all-to-all-done.4.back_ref, s32[8,2048]{1,0:T(8,128)S(1)} %get-tuple-element.60.info_ref, s32[128,128]{1,0:T(8,128)S(1)} %get-tuple-element.61.table_ref), custom_call_target="tpu_custom_call" | custom-call | tf_op jit(solution)/shard_map/answers/pallas_call | solution.py:424
  101.8 0.0 copy-done
  101.8 0.0 copy-done.1
  101.8 0.0 copy-done.2
  101.8 0.2 conditional.1
Async XLA Ops:
  81.9 19.9 %copy-start = (s32[2048]{0:T(1024)S(1)}, s32[2048]{0:T(1024)}, u32[]{:S(2)}) copy-start(s32[2048]{0:T(1024)} %param.8) | copy-start | bytes 24580
  81.9 19.9 %copy-start.1 = (s32[2048]{0:T(1024)S(1)}, s32[2048]{0:T(1024)}, u32[]{:S(2)}) copy-start(s32[2048]{0:T(1024)} %param.9) | copy-start | bytes 24580
  81.9 19.9 %copy-start.2 = (s32[128]{0:T(128)S(1)}, s32[128]{0:T(128)}, u32[]{:S(2)}) copy-start(s32[128]{0:T(128)} %param.10) | copy-start | bytes 1540
  88.4 12.3 %all-to-all-start.4 = ((bf16[32,8,256]{2,1,0:T(8,128)(2,1)}), bf16[32,8,256]{2,1,0:T(8,128)(2,1)S(1)}, u32[]{:S(2)}, u32[]{:S(2)}) async-start(bf16[32,8,256]{2,1,0:T(8,128)(2,1)} %get-tuple-element.59), calls=%async_computation.4 | async-start | bytes 262144 | tf_op jit(solution)/shard_map/all_to_all | solution.py:361
